TPU v7x, 32 devices: a whole 2x2x4 slice. The times are simulated.
32 devices in a mesh: req: 8 (over y, x, core), mlp: 4 (over z).
Axes of the slice: x: 2, y: 2, z: 4, core: 2. Of those that a mesh axis runs over, the one named last changes fastest.
Arguments:
- hidden_in: bfloat16 [16, 512, 2048], P('req'), may hold values from -6 to 6
- lengths: int32 [16], replicated, may hold values from 1 to 512, 4096 in all
- slot_request: int32 [16], replicated, may hold values from 0 to 15, each once
- adapter_of: int32 [16], replicated, may hold values from 0 to 63, as said below
- adapter_slot: int32 [64], replicated, may hold values from 0 to 63, each once
- norm_gain_attn: float32 [2048], replicated, may hold values from 0.5 to 1.5
- norm_gain_mlp: float32 [2048], replicated, may hold values from 0.5 to 1.5
- final_gain: float32 [2048], replicated, may hold values from 0.5 to 1.5
- w_qkv: bfloat16 [2048, 3, 2048], P(None, None, 'mlp')
- w_out: bfloat16 [2048, 2048], P('mlp'), may hold values from -0.125 to 0.125
- w_gateup: bfloat16 [2048, 2, 4096], P('req', None, 'mlp'), may hold values from -0.125 to 0.125
- w_down: bfloat16 [4096, 2048], P('mlp', 'req'), may hold values from -0.09375 to 0.09375
- adapter_down: bfloat16 [64, 16, 2048], P('req'), may hold values from -0.125 to 0.125
- adapter_up: bfloat16 [64, 16, 2048], P('req', None, 'mlp'), may hold values from -1.5 to 1.5
- vocab: bfloat16 [49152, 2048], P(('req', 'mlp')), may hold values from -0.375 to 0.375
Outputs:
- out_hidden: bfloat16 [16, 512, 2048], P('req')
- request_norm: float32 [16], replicated
- request_peak: float32 [16], replicated
Inputs may be any that keep to these rules, and one draw needn't show every extreme that they name: Some request has exactly 512 tokens, and all lengths together sum to 4096. `slot_request`: each request sits in exactly one slot. `adapter_of`: exactly 16 distinct adapters are named. `adapter_slot`: each adapter sits in exactly one row of the adapter tables.
All inputs are finite; a program needn't handle non-finite values.
Results may differ from a plain program's by a relative error of at most 0.018.
Values may be sent and summed in bfloat16 or wider, within the bound.
No kernel may reach another device: no remote copies, remote signals or barrier semaphores. Data moves between devices by JAX's collectives and lax.ppermute only.
A program may use at most 128 MiB of HBM per device.

v0:
```python
import functools
import math

import jax
import jax.numpy as jnp
import numpy as np
from jax import lax
from jax.experimental import pallas as pl
from jax.experimental.pallas import tpu as pltpu
from jax.sharding import PartitionSpec as P

HEAD_WIDTH = 64
EPSILON = 1e-05
ROPE_BASE = 130000.0
ADAPTER_SCALE = 2.0
MASKED = -1e30
F32, BF16 = jnp.float32, jnp.bfloat16
UNIT = 256
CLASSES = [(7, 5, 0), (8, 5, 0), (8, 6, 0), (8, 8, 64)]
MIB = 1024 * 1024

ME, Z, CORE, CLASS, TABLES = 0, 1, 2, 3, 8
LAST_ROWS = 16
ANY = pl.BlockSpec(memory_space=pl.ANY)
SMEM = pl.BlockSpec(memory_space=pltpu.SMEM)


def nt(a, b):
    return lax.dot_general(a, b, (((1,), (1,)), ((), ())), preferred_element_type=F32)


def nn(a, b):
    return jnp.dot(a, b, preferred_element_type=F32)


def call(
    kernel, grid, ins, outs, shapes, scratch=(), flops=0, nbytes=0, aliases=None, vmem=16
):
    spec = pltpu.PrefetchScalarGridSpec(
        num_scalar_prefetch=1, grid=grid, in_specs=ins, out_specs=outs, scratch_shapes=scratch
    )
    return pl.pallas_call(
        kernel,
        grid_spec=spec,
        out_shape=shapes,
        input_output_aliases=aliases or {},
        compiler_params=pltpu.CompilerParams(vmem_limit_bytes=vmem * MIB),
        cost_estimate=pl.CostEstimate(
            flops=int(flops), bytes_accessed=int(nbytes), transcendentals=0
        ),
    )


def whole(shape):
    zeros = (0,) * len(shape)
    return pl.BlockSpec(tuple(shape), lambda *_: zeros)


def rope_tables(length):
    half = HEAD_WIDTH // 2
    frequency = np.float32(ROPE_BASE) ** (-(np.arange(half, dtype=np.float32) * 2.0 / HEAD_WIDTH))
    angles = np.arange(length, dtype=np.float32)[:, None] * frequency.astype(np.float32)[None, :]
    angles = angles.astype(np.float32)
    cosine, sine = np.cos(angles), np.sin(angles)
    return (
        np.concatenate([cosine] * 4, axis=1).astype(np.float32),
        np.concatenate([-sine, sine, -sine, sine], axis=1).astype(np.float32),
    )


def rotate(block, cosine, sine):
    lane = lax.broadcasted_iota(jnp.int32, block.shape, 1)
    front = (lane % HEAD_WIDTH) < HEAD_WIDTH // 2
    partner = jnp.where(
        front, pltpu.roll(block, 128 - HEAD_WIDTH // 2, 1), pltpu.roll(block, HEAD_WIDTH // 2, 1)
    )
    return block * cosine + partner * sine


def live_at(slots, h, g):
    return TABLES + slots + h * 4 * slots + g


def place_at(slots, h, g):
    return TABLES + slots + h * 4 * slots + 2 * slots + g


def setup_kernel(
    slots, half, classes, me_ref, z_ref, lengths, slot_request, adapter_of, adapter_slot, down, up,
    info, *outs
):
    table_rows, _, width = down.shape
    me, z = me_ref[0], z_ref[0]
    core, chip = lax.rem(me, 2), lax.div(me, 2)
    chip_slots = 2 * slots
    info[ME], info[Z], info[CORE] = me, z, core

    def split(slot):
        live = lengths[slot_request[slot]]
        first = jnp.minimum(live, half)
        return first, live - first

    def aligned(live):
        return lax.div(live + 15, 16) * 16

    most = [jnp.int32(0), jnp.int32(0)]
    for c in range(slot_request.shape[0] // chip_slots):
        total = [jnp.int32(0), jnp.int32(LAST_ROWS)]
        for g in range(chip_slots):
            for h, live in enumerate(split(c * chip_slots + g)):
                total[h] = total[h] + aligned(live)
        most = [jnp.maximum(most[h], total[h]) for h in range(2)]
    choice = jnp.int32(len(classes) - 1)
    for i in reversed(range(len(classes) - 1)):
        fits = (most[0] <= 2 * classes[i][0]) & (most[1] <= 2 * classes[i][1])
        choice = jnp.where(fits, i, choice)
    info[CLASS] = choice
    total = [jnp.int32(0), jnp.int32(LAST_ROWS)]
    for g in range(chip_slots):
        for h, live in enumerate(split(chip * chip_slots + g)):
            info[live_at(slots, h, g)] = live
            info[place_at(slots, h, g)] = total[h]
            total[h] = total[h] + aligned(live)
    for s in range(slots):
        info[TABLES + s] = adapter_slot[adapter_of[slot_request[me * slots + s]]]
    for j, out in enumerate(outs):
        for s in range(slots):
            slot = (me ^ j) * slots + s
            row = lax.rem(adapter_slot[adapter_of[slot_request[slot]]], table_rows)
            out[s, :, :width] = down[row]
            out[s, :, width:] = up[row]


def merge_kernel(info, gate_up, down, out):
    depth, units = down.shape[1], down.shape[0]
    for b in range(units // UNIT):
        at = slice(b * UNIT, (b + 1) * UNIT)
        out[b, 0:depth] = gate_up[:, 0, at]
        out[b, depth : 2 * depth] = gate_up[:, 1, at]
        out[b, 2 * depth :] = down[at, :] if depth == UNIT else down[at, :].T


def project_kernel(
    info, x_ref, gain_ref, w_ref, cos_ref, sin_ref, k_ref, v_ref, q_ref, normed_ref
):
    slots, rows, width = x_ref.shape
    group = 64
    for s in range(slots):
        for i in range(rows // group):
            x = x_ref[s, i * group : (i + 1) * group].astype(F32)
            mean = jnp.mean(x * x, axis=-1, keepdims=True)
            at = slice(s * rows + i * group, s * rows + (i + 1) * group)
            normed_ref[at] = (x * lax.rsqrt(mean + EPSILON) * gain_ref[...]).astype(BF16)
    product = nn(normed_ref[...], w_ref[1])
    for s in range(slots):
        at = slice(s * rows, (s + 1) * rows)
        for g in range(product.shape[1] // 128):
            lanes = slice(g * 128, g * 128 + 128)
            k_ref[at, lanes] = rotate(product[at, lanes], cos_ref[...], sin_ref[...]).astype(BF16)
    v_ref[...] = nn(normed_ref[...], w_ref[2]).astype(BF16)
    q_ref[...] = nn(normed_ref[...], w_ref[0])


def attend_kernel(slots, table_rows, n, h, info, q_ref, normed_ref, cos_ref, sin_ref, *rest):
    keys, values = rest[: h + 1], rest[h + 1 : 2 * h + 2]
    received, (out_ref, queries) = rest[2 * h + 2 : 2 * h + 2 + (n if h == 0 else 1)], rest[-2:]
    s = pl.program_id(0)
    length, columns = q_ref.shape
    width = normed_ref.shape[1]
    if h == 0:
        out_ref, picked, queries, sem = rest[-4:]
        factors = picked.at[0]
        source = info[ME] ^ lax.div(info[TABLES + s], table_rows)
        for j in range(n):

            @pl.when(source == j)
            def _(j=j):
                pltpu.make_async_copy(received[j].at[s], factors, sem.at[0]).start()

        pltpu.make_async_copy(received[0].at[s], factors, sem.at[0]).wait()
    else:
        factors = received[0].at[0]
    low_rank = nt(normed_ref[...], factors[:, :width]).astype(BF16)
    raised = nn(low_rank, factors[:, width:])
    full = q_ref[...] + ADAPTER_SCALE * raised
    for g in range(columns // 128):
        lanes = slice(g * 128, g * 128 + 128)
        queries[:, lanes] = rotate(full[:, lanes], cos_ref[...], sin_ref[...]).astype(BF16)
    step = length
    scale = HEAD_WIDTH ** (-0.5) * math.log2(math.e)

    def pair(g):
        lanes = slice(g * 128, g * 128 + 128)
        for b in range(length // step):
            end = (b + 1) * step
            q = queries[b * step : end, lanes]
            first = lax.broadcasted_iota(jnp.int32, q.shape, 1) < HEAD_WIDTH
            zero = jnp.zeros_like(q)
            both = jnp.concatenate([jnp.where(first, q, zero), jnp.where(first, zero, q)], axis=0)
            scores = nt(both, keys[h][0:end, lanes]) * scale
            row = lax.broadcasted_iota(jnp.int32, scores.shape, 0) % step + b * step
            col = lax.broadcasted_iota(jnp.int32, scores.shape, 1)
            scores = [jnp.where(col <= row, scores, MASKED)]
            used = [values[h][0:end, lanes]]
            for before in range(h):
                scores.append(nt(both, keys[before][:, lanes]) * scale)
                used.append(values[before][:, lanes])
            top = functools.reduce(
                jnp.maximum, [jnp.max(part, axis=1, keepdims=True) for part in scores]
            )
            weights = [jnp.exp2(part - top) for part in scores]
            total = sum(jnp.sum(part, axis=1, keepdims=True) for part in weights)
            mixed = sum(nn(part.astype(BF16), value) for part, value in zip(weights, used))
            mixed = mixed / total
            out_ref[b * step : end, lanes] = jnp.where(first, mixed[:step], mixed[step:]).astype(
                BF16
            )

    for g in range(columns // 128):
        pair(g)


def targets(info, row, slots, h, half, core, stride, start):
    place = jnp.full(row.shape, -1, jnp.int32)
    for s in range(slots):
        g = core * slots + s
        live = info[live_at(slots, h, g)]
        at = info[place_at(slots, h, g)]
        inside = (row >= at) & (row < at + live)
        place = jnp.where(inside, row - at + s * stride + start, place)
    return place


def last_targets(info, row, slots, half, core, h, stride, start):
    place = jnp.full(row.shape, -1, jnp.int32)
    for s in range(slots):
        g = core * slots + s
        second = info[live_at(slots, 1, g)]
        live = info[live_at(slots, 0, g)] if h == 0 else second
        there = (second > 0) if h == 1 else (second == 0)
        place = jnp.where((row == g) & there, s * stride + start + live - 1, place)
    return place


def one_hot(place, columns):
    col = lax.broadcasted_iota(jnp.int32, (place.shape[0], columns), 1)
    return jnp.where(col == place, 1.0, 0.0).astype(BF16)


def hidden_kernel(slots, nz, sizes, info, hidden_ref, *outs):
    count = len(sizes)
    tokens = hidden_ref.shape[0]
    length = tokens // slots
    half = length // 2
    core = info[CORE]
    for h in range(count):
        quarter = sizes[h] // nz
        for whose in range(2):
            target_core = core if whose == 0 else 1 - core
            base = target_core * sizes[h] + info[Z] * quarter
            row = lax.broadcasted_iota(jnp.int32, (quarter, 1), 0) + base
            place = targets(info, row, slots, h, half, core, length, h * half)
            if h == 1:
                for part in range(2):
                    late = last_targets(info, row, slots, half, core, part, length, part * half)
                    place = jnp.maximum(place, late)
            outs[whose * count + h][...] = nn(one_hot(place, tokens), hidden_ref[...]).astype(BF16)


def mix_kernel(slots, size, h, info, w_ref, *rest):
    parts, out_ref = rest[:-1], rest[-1]
    tokens = parts[0].shape[0]
    half = tokens // slots
    core = info[CORE]
    cores = (core, 1 - core)
    row = lax.broadcasted_iota(jnp.int32, (size, 1), 0) + core * size
    packed = 0.0
    for whose in range(2):
        place = targets(info, row, slots, h, half, cores[whose], half, 0)
        if h == 1:
            late = last_targets(info, row, slots, half, cores[whose], 1, half, 0)
            place = jnp.maximum(place, late)
        packed = packed + nn(one_hot(place, tokens), parts[whose][...])
    if h == 1:
        front = 0.0
        for whose in range(2):
            place = last_targets(info, row[:LAST_ROWS], slots, half, cores[whose], 0, half, 0)
            front = front + nn(one_hot(place, tokens), parts[2 + whose][...])
        packed = jnp.concatenate([packed[:LAST_ROWS] + front, packed[LAST_ROWS:]], axis=0)
    product = nn(packed.astype(BF16), w_ref[...]).astype(BF16)
    out_ref[...] = product.reshape(out_ref.shape)


def stream_kernel(info, own, other, gain, *rest):
    terms, (stream_ref, normed_ref) = rest[:-2], rest[-2:]
    mixed = sum(term[...].astype(F32) for term in terms)
    hidden = own[...].astype(F32) + other[...].astype(F32)
    stream = (hidden + mixed).astype(BF16)
    stream_ref[...] = stream
    x = stream.astype(F32)
    mean = jnp.mean(x * x, axis=-1, keepdims=True)
    normed_ref[...] = (x * lax.rsqrt(mean + EPSILON) * gain[...]).astype(BF16)


def finish_kernel(slots, size, h, count, info, stream, gain, *rest):
    terms, (out_ref, sums_ref), lasts = rest[:count], rest[count : count + 2], rest[count + 2 :]
    quarter, width = stream.shape
    chip_slots = 2 * slots
    total = sum(term[...].astype(F32) for term in terms)
    result = stream[...].astype(F32) + total
    base = info[CORE] * size + info[Z] * quarter
    row = lax.broadcasted_iota(jnp.int32, (quarter, 1), 0) + base
    keep = (row < chip_slots) if h == 1 else (row < 0)
    belongs = []
    for g in range(chip_slots):
        live, at = info[live_at(slots, h, g)], info[place_at(slots, h, g)]
        inside = (row >= at) & (row < at + live)
        belongs.append(inside)
        keep = keep | inside
    rounded = jnp.where(keep, result, 0.0).astype(BF16)
    out_ref[...] = rounded
    wide = rounded.astype(F32)
    squares = jnp.sum(wide * wide, axis=1, keepdims=True)
    lane = lax.broadcasted_iota(jnp.int32, sums_ref.shape, 1)
    first_slot = lax.div(info[ME], 2) * chip_slots
    sums = jnp.zeros(sums_ref.shape, F32)
    for g in range(chip_slots):
        part = jnp.sum(jnp.where(belongs[g], squares, 0.0))
        sums = jnp.where(lane == first_slot + g, part, sums)
    sums_ref[...] = sums
    for last_ref in lasts:
        last_ref[...] = jnp.zeros(last_ref.shape, BF16)
        front = wide[:LAST_ROWS]
        mean = jnp.mean(front * front, axis=-1, keepdims=True)
        last = (front * lax.rsqrt(mean + EPSILON) * gain[...]).astype(BF16)
        slot = lax.broadcasted_iota(jnp.int32, (last_ref.shape[0], LAST_ROWS), 0) - first_slot
        kept = lax.broadcasted_iota(jnp.int32, slot.shape, 1)
        pick = jnp.where((slot == kept) & (kept < chip_slots), 1.0, 0.0).astype(BF16)

        @pl.when(base == 0)
        def _():
            last_ref[...] = nn(pick, last).astype(BF16)


def in_order(nz, z, own, rights, lefts, out, sems):
    quarter = own.shape[0]

    def copy(piece, place):
        return pltpu.make_async_copy(
            piece, out.at[pl.ds(place * quarter, quarter)], sems.at[place]
        )

    for place in range(nz):

        @pl.when(z == place)
        def _(place=place):
            copy(own, place).start()

        for d in range(1, nz):

            @pl.when(z - place == d)
            def _(place=place, d=d):
                copy(rights[d - 1], place).start()

            @pl.when(place - z == d)
            def _(place=place, d=d):
                copy(lefts[d - 1], place).start()

    for place in range(nz):
        copy(own, place).wait()


def order_kernel(nz, info, own, *rest):
    rights, lefts, (out, sems) = rest[: nz - 1], rest[nz - 1 : 2 * nz - 2], rest[2 * nz - 2 :]
    in_order(nz, info[Z], own, rights, lefts, out, sems)


def unpack_kernel(slots, h, info, mine, theirs, *rest):
    out, packed, sems = rest[-3:]
    s = pl.program_id(0)
    size = mine.shape[0]
    core = info[CORE]

    @pl.when(s == 0)
    def _():
        copies = [
            pltpu.make_async_copy(
                piece,
                packed.at[pl.ds(pl.multiple_of(place * size, 16), size)],
                sems.at[i],
            )
            for i, (piece, place) in enumerate(((mine, core), (theirs, 1 - core)))
        ]
        for copy in copies:
            copy.start()
        for copy in copies:
            copy.wait()

    g = core * slots + s
    live, at = info[live_at(slots, h, g)], info[place_at(slots, h, g)]
    rows = packed[pl.ds(pl.multiple_of(at, 16), out.shape[0])]
    row = lax.broadcasted_iota(jnp.int32, (out.shape[0], 1), 0)
    out[...] = jnp.where(row < live, rows, jnp.zeros((), BF16))


def unit_kernel(nz, info, own, *rest):
    rights, lefts = rest[: nz - 1], rest[nz - 1 : 2 * nz - 2]
    w_ref, out_ref, x, acc, sems = rest[2 * nz - 2 :]
    b = pl.program_id(0)
    n, _, depth, columns = w_ref.shape
    depth = depth // 3
    width = x.shape[1]

    @pl.when(b == 0)
    def _():
        in_order(nz, info[Z], own, rights, lefts, x, sems)
        acc[...] = jnp.zeros(acc.shape, F32)

    gate = nn(x[...], w_ref[:, 0, 0:depth].reshape(width, columns))
    up = nn(x[...], w_ref[:, 0, depth : 2 * depth].reshape(width, columns))
    active = (gate / (1.0 + jnp.exp(-gate)) * up).astype(BF16)
    if depth == UNIT:
        for r in range(n):
            at = slice(r * depth, (r + 1) * depth)
            acc[:, at] += nn(active, w_ref[r, 0, 2 * depth :])
    else:
        acc[...] += nt(active, w_ref[:, 0, 2 * depth :].reshape(width, columns))

    @pl.when(b == pl.num_programs(0) - 1)
    def _():
        out_ref[...] = acc[...].astype(BF16).reshape(out_ref.shape)


def peak_kernel(info, every, vocab, out):
    b = pl.program_id(0)
    best = jnp.max(nt(vocab[...], every[...]), axis=0, keepdims=True)
    best = jnp.broadcast_to(best, (out.shape[0], every.shape[0]))

    @pl.when(b == 0)
    def _():
        out[...] = jnp.zeros(out.shape, F32)
        out[:, : every.shape[0]] = best

    @pl.when(b > 0)
    def _():
        out[:, : every.shape[0]] = jnp.maximum(out[:, : every.shape[0]], best)


def following(info, array):
    return lax.optimization_barrier((info, array))[0]


class Order:
    def __init__(self):
        self.before = None

    def __call__(self, *arrays):
        if self.before is not None:
            *arrays, _ = lax.optimization_barrier((*arrays, self.before))
        elif len(arrays) > 1:
            arrays = lax.optimization_barrier(arrays)
        self.before = arrays[0]
        return arrays


def reduce_start(parts, order, z, nz):
    last = nz - 1
    index = jnp.where(z == 0, last, 0)
    (message,) = order(lax.dynamic_index_in_dim(parts, index, 0, keepdims=False))
    came = lax.ppermute(message, "mlp", [(0, 1), (last, last - 1)])
    return message, [came, came]


def reduce_step(parts, came, s, order, z, nz):
    def take(index):
        return lax.dynamic_index_in_dim(parts, jnp.clip(index, 0, nz - 1), 0, keepdims=False)

    last = nz - 1
    *came, _ = lax.optimization_barrier((*came, order.before))
    right, left = take(nz - s + z), take(s + z - nz)
    if s == 2:
        right = jnp.where(z == 0, right, right + came[0])
        left = jnp.where(z == last, left, left + came[1])
    else:
        right, left = right + came[0], left + came[1]
    right, left = order(right, left)
    return [
        lax.ppermute(right, "mlp", [(i, i + 1) for i in range(s)]),
        lax.ppermute(left, "mlp", [(last - i, last - 1 - i) for i in range(s)]),
    ]


def spread_step(rights, lefts, s, order, z, nz):
    last = nz - 1
    if s < last:
        right, left = order(rights[-1], lefts[-1])
        rights.append(lax.ppermute(right, "mlp", [(i, i + 1) for i in range(s - 1, last)]))
        lefts.append(lax.ppermute(left, "mlp", [(i + 1, i) for i in range(0, nz - s)]))
    else:
        (message,) = order(jnp.where(z == last - 1, rights[-1], lefts[-1]))
        message = lax.ppermute(message, "mlp", [(last - 1, last), (1, 0)])
        rights.append(message)
        lefts.append(message)


def hops(n, nz):
    bit = 2
    while bit < n * nz:
        if bit < n:
            yield "req", [(i, i ^ bit) for i in range(n)]
        else:
            yield "mlp", [(i, i ^ (bit // n)) for i in range(nz)]
        bit *= 2
    yield "req", [(i, i ^ 1) for i in range(n)]


def layer(sizes, sizes_n, table_rows, lengths, slot_request, info, hidden, gains, w_qkv, w_out, w_gateup, w_down, picked, vocab):
    n, nz = sizes_n
    z = lax.axis_index("mlp")
    gain_attn, gain_mlp, final_gain = gains
    slots, length, width = hidden.shape
    rows, half = slots * length, length // 2
    columns = w_qkv.shape[2]
    units = w_down.shape[0]
    slots_all = n * slots
    swap = [(i, i ^ 1) for i in range(n)]
    factor_shape = picked[0].shape
    received = [picked[0]] + [
        lax.ppermute(picked[j], "req", [(i, i ^ j) for i in range(n)]) for j in range(1, n)
    ]

    cosine, sine = rope_tables(length)
    part_rows = slots * half
    projected = []
    for h in range(2):
        table = pl.BlockSpec((half, 128), lambda i, _, h=h: (h, 0))
        projected.append(
            call(
                project_kernel,
                (1,),
                [
                    pl.BlockSpec((slots, half, width), lambda i, _, h=h: (0, h, 0)),
                    whole((1, width)),
                    whole(w_qkv.shape),
                    table,
                    table,
                ],
                [whole((part_rows, columns))] * 3 + [whole((part_rows, width))],
                [
                    jax.ShapeDtypeStruct((part_rows, columns), BF16),
                    jax.ShapeDtypeStruct((part_rows, columns), BF16),
                    jax.ShapeDtypeStruct((part_rows, columns), F32),
                    jax.ShapeDtypeStruct((part_rows, width), BF16),
                ],
                vmem=32,
                flops=2 * part_rows * width * 3 * columns,
                nbytes=2 * (2 * part_rows * width + 3 * width * columns),
            )(info, hidden, gain_attn, w_qkv, cosine, sine)
        )

    quarters = [size // nz for size in sizes]
    quarter_shapes = [jax.ShapeDtypeStruct((q, width), BF16) for q in quarters]
    quarter_specs = [whole((q, width)) for q in quarters]
    attended, other, head_parts, came, order = [], [], [], [], Order()
    for h in range(2):
        by_slot = lambda w: pl.BlockSpec((half, w), lambda s, _: (s, 0))
        table = pl.BlockSpec((half, 128), lambda s, _, h=h: (h, 0))
        by_factor = pl.BlockSpec((1,) + factor_shape[1:], lambda s, _: (s, 0, 0))
        own_factors = h == 0
        mixed = call(
            functools.partial(attend_kernel, slots, table_rows, n, h),
            (slots,),
            [by_slot(columns), by_slot(width), table, table]
            + [by_slot(columns)] * (2 * h + 2)
            + ([ANY] * n if own_factors else [by_factor]),
            [by_slot(columns)] + [by_factor] * own_factors,
            [jax.ShapeDtypeStruct((part_rows, columns), BF16)]
            + [jax.ShapeDtypeStruct(factor_shape, BF16)] * own_factors,
            [pltpu.VMEM((half, columns), BF16)] + [pltpu.SemaphoreType.DMA((1,))] * own_factors,
            flops=8 * part_rows * (h + 1) * half * columns,
            nbytes=2 * part_rows * (width + 6 * columns),
        )(
            following(info, projected[1][1] if own_factors else first),
            projected[h][2],
            projected[h][3],
            cosine,
            sine,
            *[projected[i][0] for i in range(h + 1)],
            *[projected[i][1] for i in range(h + 1)],
            *received,
        )
        attended.append(mixed[0])
        if own_factors:
            received = mixed[1:]
        other.append(lax.ppermute(attended[h], "req", swap))
        size, q = sizes[h], quarters[h]
        part_shape = jax.ShapeDtypeStruct((nz, q, width), BF16)
        parts = [attended[h], other[h]] + ([attended[0], other[0]] if h == 1 else [])
        mixed = call(
            functools.partial(mix_kernel, slots, size, h),
            (1,),
            [whole(w_out.shape)] + [whole((part_rows, columns))] * len(parts),
            whole(part_shape.shape),
            part_shape,
            vmem=24,
            flops=2 * size * columns * (2 * part_rows + width),
            nbytes=2 * (columns * (2 * part_rows + width) + size * width),
        )(info, w_out, *parts)
        head_parts.append(mixed)
        first, came_h = reduce_start(mixed, order, z, nz)
        came.append(came_h)

    depth = w_down.shape[1]
    merged = call(
        merge_kernel,
        (1,),
        [whole(w_gateup.shape), whole(w_down.shape)],
        whole((units // UNIT, 3 * depth, UNIT)),
        jax.ShapeDtypeStruct((units // UNIT, 3 * depth, UNIT), BF16),
        nbytes=12 * depth * units,
    )(following(info, head_parts[0]), w_gateup, w_down)
    weights = lax.all_gather(merged, "req", axis=0)

    shared = call(
        functools.partial(hidden_kernel, slots, nz, sizes),
        (1,),
        [whole((rows, width))],
        quarter_specs * 2,
        quarter_shapes * 2,
        vmem=20,
        flops=4 * sum(quarters) * rows * width,
        nbytes=2 * rows * width,
    )(following(info, head_parts[0]), hidden.reshape(rows, width))
    hidden_own = shared[:2]
    hidden_other = [lax.ppermute(piece, "req", swap) for piece in shared[2:]]

    parts = head_parts
    for s in range(2, nz):
        came = [reduce_step(parts[h], came[h], s, order, z, nz) for h in range(2)]
    streams, rights, lefts = [], [], []
    for h in range(2):
        q, spec = quarters[h], quarter_specs[h]
        terms = [lax.dynamic_index_in_dim(parts[h], z, 0, keepdims=False), *came[h]]
        stream, mid = call(
            stream_kernel,
            (1,),
            [spec] * 2 + [whole((1, width))] + [spec] * len(terms),
            [spec, spec],
            [quarter_shapes[h]] * 2,
            nbytes=14 * q * width,
        )(following(info, head_parts[1]), hidden_own[h], hidden_other[h], gain_mlp, *terms)
        streams.append(stream)
        rights.append([mid])
        lefts.append([mid])
        spread_step(rights[h], lefts[h], 1, order, z, nz)
    for s in range(2, nz):
        for h in range(2):
            spread_step(rights[h], lefts[h], s, order, z, nz)

    parts, came = [], []
    for h in range(2):
        q, size = quarters[h], sizes[h]
        part_shape = jax.ShapeDtypeStruct((nz, q, width), BF16)
        unit_parts = call(
            functools.partial(unit_kernel, nz),
            (units // UNIT,),
            [ANY] * (2 * nz - 1)
            + [pl.BlockSpec((n, 1) + weights.shape[2:], lambda b, _: (0, b, 0, 0))],
            whole(part_shape.shape),
            part_shape,
            [
                pltpu.VMEM((size, width), BF16),
                pltpu.VMEM((size, width), F32),
                pltpu.SemaphoreType.DMA((nz,)),
            ],
            vmem=28,
            flops=6 * size * width * units,
            nbytes=2 * weights.size,
        )(info, *rights[h], *lefts[h][1:], weights)
        parts.append(unit_parts)
        came.append(reduce_start(unit_parts, order, z, nz)[1])
    for s in range(2, nz):
        came = [reduce_step(parts[h], came[h], s, order, z, nz) for h in range(2)]

    sums, rights, lefts = [], [], []
    for h in range(2):
        q, size, spec = quarters[h], sizes[h], quarter_specs[h]
        terms = [lax.dynamic_index_in_dim(parts[h], z, 0, keepdims=False), *came[h]]
        extra = [(slots_all, width)] if h == 1 else []
        finished = call(
            functools.partial(finish_kernel, slots, size, h, len(terms)),
            (1,),
            [spec, whole((1, width))] + [spec] * len(terms),
            [spec, whole((8, 128))] + [whole(e) for e in extra],
            [quarter_shapes[h], jax.ShapeDtypeStruct((8, 128), F32)]
            + [jax.ShapeDtypeStruct(e, BF16) for e in extra],
            nbytes=10 * q * width,
        )(info, streams[h], final_gain, *terms)
        sums.append(finished[1])
        rights.append([finished[0]])
        lefts.append([finished[0]])
        spread_step(rights[h], lefts[h], 1, order, z, nz)
    every = finished[2]
    steps = list(hops(n, nz))

    def share(step):
        nonlocal every
        if step < len(steps):
            (message,) = order(every)
            every = every + lax.ppermute(message, *steps[step])

    share(0)
    done = 1
    for s in range(2, nz):
        for h in range(2):
            spread_step(rights[h], lefts[h], s, order, z, nz)
            if s < nz - 1:
                share(done)
                done += 1
    while done < len(steps):
        share(done)
        done += 1

    def ordered(h):
        size = sizes[h]
        rights[h][-1], lefts[h][-1], _ = lax.optimization_barrier(
            (rights[h][-1], lefts[h][-1], order.before)
        )
        mine = call(
            functools.partial(order_kernel, nz),
            (1,),
            [ANY] * (2 * nz - 1),
            whole((size, width)),
            jax.ShapeDtypeStruct((size, width), BF16),
            [pltpu.SemaphoreType.DMA((nz,))],
            nbytes=4 * size * width,
        )(info, *rights[h], *lefts[h][1:])
        (mine,) = order(mine)
        return mine, lax.ppermute(mine, "req", swap)

    def unpacked(h, mine, theirs, held):
        size = sizes[h]
        return call(
            functools.partial(unpack_kernel, slots, h),
            (slots,),
            [ANY, ANY] + [ANY] * len(held),
            pl.BlockSpec((half, width), lambda s, _, h=h: (2 * s + h, 0)),
            jax.ShapeDtypeStruct((rows, width), BF16),
            [pltpu.VMEM((2 * size + half, width), BF16), pltpu.SemaphoreType.DMA((2,))],
            nbytes=2 * rows * width,
            aliases={3: 0} if held else None,
        )(info, mine, theirs, *held)

    block = vocab.shape[0] // 3
    peaks = call(
        peak_kernel,
        (3,),
        [whole(every.shape), pl.BlockSpec((block, width), lambda b, _: (b, 0))],
        whole((8, 128)),
        jax.ShapeDtypeStruct((8, 128), F32),
        flops=2 * slots_all * vocab.size,
        nbytes=2 * vocab.size,
    )(info, every, vocab)
    both = jnp.concatenate([sums[0] + sums[1], peaks], axis=0)
    row = lax.broadcasted_iota(jnp.int32, both.shape, 0)

    def combine(both, hop):
        (message,) = order(both)
        arrived = lax.ppermute(message, *hop)
        return jnp.where(row < 8, both + arrived, jnp.maximum(both, arrived))

    early = ordered(0)
    late = ordered(1)
    out = unpacked(0, *early, [])
    for hop in steps:
        both = combine(both, hop)
    out = unpacked(1, *late, [out])
    norm_sums, peaks = both[0, :slots_all], both[8, :slots_all]
    requests = jnp.arange(slots_all, dtype=jnp.int32)
    owners = slot_request[None, :] == requests[:, None]
    norm_sums = jnp.sum(jnp.where(owners, norm_sums[None, :], 0.0), axis=1)
    request_norm = jnp.sqrt(norm_sums / (lengths.astype(F32) * width))
    request_peak = jnp.sum(jnp.where(owners, peaks[None, :], 0.0), axis=1)
    return out.reshape(slots, length, width), request_norm, request_peak


def per_device(sizes_n, *arrays):
    (hidden, lengths, slot_request, adapter_of, adapter_slot, gain_attn, gain_mlp, final_gain) = (
        arrays[:8]
    )
    (w_qkv, w_out, w_gateup, w_down, adapter_down, adapter_up, vocab) = arrays[8:]
    n, nz = sizes_n
    slots, length, width = hidden.shape
    me, z = lax.axis_index("req"), lax.axis_index("mlp")
    part_rows = slots * length // 2
    classes = [
        (part_rows * a // 8, part_rows * b // 8 + c) for a, b, c in CLASSES
    ]
    factor_shape = (slots, adapter_down.shape[1], width + adapter_up.shape[2])
    info, *picked = pl.pallas_call(
        functools.partial(setup_kernel, slots, length // 2, classes),
        in_specs=[SMEM] * 6 + [pl.BlockSpec(memory_space=pltpu.VMEM)] * 2,
        out_specs=[SMEM] + [pl.BlockSpec(memory_space=pltpu.VMEM)] * n,
        out_shape=[jax.ShapeDtypeStruct((TABLES + 9 * slots,), jnp.int32)]
        + [jax.ShapeDtypeStruct(factor_shape, BF16)] * n,
        compiler_params=pltpu.CompilerParams(vmem_limit_bytes=60 * MIB),
    )(
        me.reshape(1), z.reshape(1), lengths, slot_request, adapter_of, adapter_slot,
        adapter_down, adapter_up,
    )
    operands = (
        lengths,
        slot_request,
        info,
        hidden,
        tuple(g.reshape(1, width) for g in (gain_attn, gain_mlp, final_gain)),
        w_qkv.transpose(1, 0, 2),
        w_out,
        w_gateup,
        w_down,
        tuple(picked),
        vocab,
    )
    branches = [
        functools.partial(layer, sizes, sizes_n, adapter_down.shape[0]) for sizes in classes
    ]
    if len(branches) == 1:
        return branches[0](*operands)
    return lax.switch(info[CLASS], branches, *operands)


def solution(mesh):
    return jax.shard_map(
        functools.partial(per_device, (mesh.shape["req"], mesh.shape["mlp"])),
        mesh=mesh,
        in_specs=(
            P("req", None, None),
            P(),
            P(),
            P(),
            P(),
            P(),
            P(),
            P(),
            P(None, None, "mlp"),
            P("mlp", None),
            P("req", None, "mlp"),
            P("mlp", "req"),
            P("req", None, None),
            P("req", None, "mlp"),
            P(("req", "mlp"), None),
        ),
        out_specs=(P("req", None, None), P(), P()),
        check_vma=False,
    )
```

profile of v0, /device:TPU:0, one launch (start us, length us, event | category | flops | bytes accessed | tf_op | source)
XLA Modules:
  0.0 388.1 jit_solution(16757221867080724707)
XLA Ops:
  10.5 370.1 %conditional.1 = (bf16[2,512,2048]{2,1,0:T(8,128)(2,1)}, f32[16]{0:T(128)}, f32[16]{0:T(128)}) conditional(s32[]{:T(128)} %bitcast.118, (s32[26]{0:T(128)S(1)}, bf16[2,512,2048]{2,1,0:T(8,128)(2,1)}, f32[1,2048]{1,0:T(1,128)}, bf16[3,2048,512]{2,1,0:T(8,128)(2,1)}, f32[512,128]{1,0:T(8,128)}, ...), branch_computations={%region_0.3_spmd, %region_3.6_spmd, %region_6.9_spmd, %region_9.12... | conditional | flops 27556188160 | bytes 611279232 | solution.py:829
  16.2 2.6 collective-permute-start.127
  20.6 8.1 %branch_2_fun.19 = (bf16[512,512]{1,0:T(8,128)(2,1)S(1)}, bf16[512,512]{1,0:T(8,128)(2,1)S(1)}, f32[512,512]{1,0:T(8,128)S(1)}, bf16[512,2048]{1,0:T(8,128)(2,1)S(1)}) custom-call(s32[26]{0:T(128)S(1)} %get-tuple-element.444.info, bf16[2,512,2048]{2,1,0:T(8,128)(2,1)} %get-tuple-element.418.x_ref, f32[1,2048]{1,0:T(1,128)} %get-tuple-element.419.gain_ref, ...), custom_call_target="tpu_custom_call" | custom-call | flops 3221225472 | bytes 10485760 | tf_op jit(solution)/shard_map/cond/branch_2_fun/pallas_call | solution.py:538
  31.1 2.6 collective-permute-start.131
  33.8 4.4 %branch_2_fun.20 = (bf16[512,512]{1,0:T(8,128)(2,1)S(1)}, bf16[512,512]{1,0:T(8,128)(2,1)S(1)}, f32[512,512]{1,0:T(8,128)S(1)}, bf16[512,2048]{1,0:T(8,128)(2,1)S(1)}) custom-call(s32[26]{0:T(128)S(1)} %get-tuple-element.444.info, bf16[2,512,2048]{2,1,0:T(8,128)(2,1)S(1)} %copy-done.134, f32[1,2048]{1,0:T(1,128)S(1)} %copy-done.140, ...), custom_call_target="tpu_custom_call" | custom-call | flops 3221225472 | bytes 10485760 | tf_op jit(solution)/shard_map/cond/branch_2_fun/pallas_call | solution.py:538
  41.7 5.9 %branch_2_fun.21 = (bf16[512,512]{1,0:T(8,128)(2,1)S(1)}, bf16[2,16,2560]{2,1,0:T(8,128)(2,1)S(1)}) custom-call(s32[26]{0:T(128)S(1)} %get-tuple-element.444.info, f32[512,512]{1,0:T(8,128)S(1)} %get-tuple-element.425.q_ref, bf16[512,2048]{1,0:T(8,128)(2,1)S(1)} %get-tuple-element.426.normed_ref, f32[512,128]{1,0:T(8,128)S(1)} %copy-done.101, ...), custom_call_target="tpu_custom_call" | custom-call | flops 536870912 | bytes 5242880 | tf_op jit(solution)/shard_map/cond/branch_2_fun/pallas_call | solution.py:570
  52.0 3.9 branch_2_fun.28
  61.2 7.9 %branch_2_fun.23.rest_0_ = bf16[512,512]{1,0:T(8,128)(2,1)} custom-call(s32[26]{0:T(128)S(1)} %get-tuple-element.444.info, f32[512,512]{1,0:T(8,128)S(1)} %copy-done.23, bf16[512,2048]{1,0:T(8,128)(2,1)S(1)} %copy-done.11, f32[512,128]{1,0:T(8,128)} %get-tuple-element.421.cos_ref, f32[512,128]{1,0:T(8,128)} %get-tuple-element.422.sin_ref, ...), custom_call_target="tpu_custom_call" | custom-call | flops 1073741824 | bytes 5242880 | tf_op jit(solution)/shard_map/cond/branch_2_fun/pallas_call | solution.py:570
  69.4 3.7 collective-permute-start.137
  75.2 3.9 branch_2_fun.24
  81.3 4.4 %collective-permute-done.137 = bf16[128,2048]{1,0:T(8,128)(2,1)S(1)} collective-permute-done((bf16[128,2048]{1,0:T(8,128)(2,1)}, bf16[128,2048]{1,0:T(8,128)(2,1)S(1)}, u32[]{:S(2)}, u32[]{:S(2)}) %collective-permute-start.137) | collective-permute-done | bytes 524320 | tf_op jit(solution)/shard_map/cond/branch_2_fun/ppermute | solution.py:470
  86.4 5.1 %collective-permute-start.140 = (bf16[128,2048]{1,0:T(8,128)(2,1)S(1)}, bf16[128,2048]{1,0:T(8,128)(2,1)S(1)}, u32[]{:S(2)}, u32[]{:S(2)}) collective-permute-start(bf16[128,2048]{1,0:T(8,128)(2,1)S(1)} %get-tuple-element.451), channel_id=1, source_target_pairs={{0,1},{1,2},{4,5},{5,6},{8,9},{9,10},{12,13},{13,14},{16,17},{17,1... | collective-permute-start | bytes 1572872 | tf_op jit(solution)/shard_map/cond/branch_2_fun/ppermute | solution.py:488
  91.5 3.1 branch_2_fun.25
  95.7 5.1 %collective-permute-start.138 = (bf16[96,2048]{1,0:T(8,128)(2,1)S(1)}, bf16[96,2048]{1,0:T(8,128)(2,1)S(1)}, u32[]{:S(2)}, u32[]{:S(2)}) collective-permute-start(bf16[96,2048]{1,0:T(8,128)(2,1)S(1)} %get-tuple-element.454), channel_id=1, source_target_pairs={{0,1},{1,2},{4,5},{5,6},{8,9},{9,10},{12,13},{13,14},{16,17},{17,1... | collective-permute-start | bytes 1179656 | tf_op jit(solution)/shard_map/cond/branch_2_fun/ppermute | solution.py:488
  100.9 4.3 %collective-permute-done.140 = bf16[128,2048]{1,0:T(8,128)(2,1)S(1)} collective-permute-done((bf16[128,2048]{1,0:T(8,128)(2,1)S(1)}, bf16[128,2048]{1,0:T(8,128)(2,1)S(1)}, u32[]{:S(2)}, u32[]{:S(2)}) %collective-permute-start.140) | collective-permute-done | bytes 524320 | tf_op jit(solution)/shard_map/cond/branch_2_fun/ppermute | solution.py:488
  106.6 5.0 %collective-permute-start.145 = (bf16[128,2048]{1,0:T(8,128)(2,1)S(1)}, bf16[128,2048]{1,0:T(8,128)(2,1)S(1)}, u32[]{:S(2)}, u32[]{:S(2)}) collective-permute-start(bf16[128,2048]{1,0:T(8,128)(2,1)S(1)} %get-tuple-element.459), channel_id=1, source_target_pairs={{0,1},{1,2},{2,3},{4,5},{5,6},{6,7},{8,9},{9,10},{10,11},{12,13},{... | collective-permute-start | bytes 1572872 | tf_op jit(solution)/shard_map/cond/branch_2_fun/ppermute | solution.py:488
  113.7 6.9 %collective-permute-done.146.rest_2_ = bf16[128,2048]{1,0:T(8,128)(2,1)S(1)} collective-permute-done((bf16[128,2048]{1,0:T(8,128)(2,1)S(1)}, bf16[128,2048]{1,0:T(8,128)(2,1)S(1)}, u32[]{:S(2)}, u32[]{:S(2)}) %collective-permute-start.146) | collective-permute-done | bytes 524320 | tf_op jit(solution)/shard_map/cond/branch_2_fun/ppermute | solution.py:489
  120.6 3.6 collective-permute-done.145.rest_1_
  126.5 5.9 %collective-permute-start.149 = (bf16[128,2048]{1,0:T(8,128)(2,1)S(1)}, bf16[128,2048]{1,0:T(8,128)(2,1)}, u32[]{:S(2)}, u32[]{:S(2)}) collective-permute-start(bf16[128,2048]{1,0:T(8,128)(2,1)S(1)} %get-tuple-element.474.own), channel_id=1, source_target_pairs={{0,1},{1,2},{2,3},{4,5},{5,6},{6,7},{8,9},{9,10},{10,11},{12,13},{... | collective-permute-start | bytes 1572872 | tf_op jit(solution)/shard_map/cond/branch_2_fun/ppermute | solution.py:497
  133.7 4.6 %collective-permute-start.142 = (bf16[96,2048]{1,0:T(8,128)(2,1)S(1)}, bf16[96,2048]{1,0:T(8,128)(2,1)S(1)}, u32[]{:S(2)}, u32[]{:S(2)}) collective-permute-start(bf16[96,2048]{1,0:T(8,128)(2,1)S(1)} %get-tuple-element.462), channel_id=1, source_target_pairs={{0,1},{1,2},{2,3},{4,5},{5,6},{6,7},{8,9},{9,10},{10,11},{12,13},{... | collective-permute-start | bytes 1179656 | tf_op jit(solution)/shard_map/cond/branch_2_fun/ppermute | solution.py:488
  138.3 11.4 %collective-permute-done.143.rest_2_ = bf16[96,2048]{1,0:T(8,128)(2,1)S(1)} collective-permute-done((bf16[96,2048]{1,0:T(8,128)(2,1)S(1)}, bf16[96,2048]{1,0:T(8,128)(2,1)S(1)}, u32[]{:S(2)}, u32[]{:S(2)}) %collective-permute-start.143) | collective-permute-done | bytes 393248 | tf_op jit(solution)/shard_map/cond/branch_2_fun/ppermute | solution.py:489
  155.1 9.7 %collective-permute-start.147 = (bf16[96,2048]{1,0:T(8,128)(2,1)S(1)}, bf16[96,2048]{1,0:T(8,128)(2,1)}, u32[]{:S(2)}, u32[]{:S(2)}) collective-permute-start(bf16[96,2048]{1,0:T(8,128)(2,1)S(1)} %get-tuple-element.473.own), channel_id=1, source_target_pairs={{0,1},{1,2},{2,3},{4,5},{5,6},{6,7},{8,9},{9,10},{10,11},{12,13},{... | collective-permute-start | bytes 1179656 | tf_op jit(solution)/shard_map/cond/branch_2_fun/ppermute | solution.py:497
  165.6 10.1 %collective-permute-done.148.rest_3_ = bf16[96,2048]{1,0:T(8,128)(2,1)} collective-permute-done((bf16[96,2048]{1,0:T(8,128)(2,1)S(1)}, bf16[96,2048]{1,0:T(8,128)(2,1)}, u32[]{:S(2)}, u32[]{:S(2)}) %collective-permute-start.148) | collective-permute-done | bytes 393248 | tf_op jit(solution)/shard_map/cond/branch_2_fun/ppermute | solution.py:498
  179.0 11.6 %collective-permute-done.152.rest_4_ = bf16[96,2048]{1,0:T(8,128)(2,1)S(1)} collective-permute-done((bf16[96,2048]{1,0:T(8,128)(2,1)}, bf16[96,2048]{1,0:T(8,128)(2,1)S(1)}, u32[]{:S(2)}, u32[]{:S(2)}) %collective-permute-start.152) | collective-permute-done | bytes 393248 | tf_op jit(solution)/shard_map/cond/branch_2_fun/ppermute | solution.py:498
  192.7 9.1 %collective-permute-done.156.rest_2_.rest_5_ = bf16[128,2048]{1,0:T(8,128)(2,1)S(1)} collective-permute-done((bf16[128,2048]{1,0:T(8,128)(2,1)S(1)}, bf16[128,2048]{1,0:T(8,128)(2,1)S(1)}, u32[]{:S(2)}, u32[]{:S(2)}) %collective-permute-start.156) | collective-permute-done | bytes 524320 | tf_op jit(solution)/shard_map/cond/branch_2_fun/ppermute | solution.py:501
  202.6 4.6 %copy-done.60 = bf16[32,768,256]{2,1,0:T(8,128)(2,1)S(1)} copy-done((bf16[32,768,256]{2,1,0:T(8,128)(2,1)S(1)}, bf16[32,768,256]{2,1,0:T(8,128)(2,1)}, u32[]{:S(2)}) %copy-start.60) | copy-done | bytes 12582936 | tf_op jit(solution)/shard_map/cond
  208.3 10.2 %branch_2_fun.30 = bf16[4,128,2048]{2,1,0:T(8,128)(2,1)S(1)} custom-call(s32[26]{0:T(128)S(1)} %get-tuple-element.444.info, bf16[128,2048]{1,0:T(8,128)(2,1)S(1)} %get-tuple-element.474.own, bf16[128,2048]{1,0:T(8,128)(2,1)} %collective-permute-done.149.rest_0_, bf16[128,2048]{1,0:T(8,128)(2,1)S(1)} %collective-permute-done.153.rest_1_, ...), custom_call_target="tpu_custom_call" | custom-call | flops 6442450944 | bytes 12582912 | tf_op jit(solution)/shard_map/cond/branch_2_fun/pallas_call | solution.py:664
  220.2 9.1 %branch_2_fun.29 = bf16[4,96,2048]{2,1,0:T(8,128)(2,1)S(1)} custom-call(s32[26]{0:T(128)S(1)} %get-tuple-element.444.info, bf16[96,2048]{1,0:T(8,128)(2,1)S(1)} %copy-done.84, bf16[96,2048]{1,0:T(8,128)(2,1)} %collective-permute-done.147.rest_0_, bf16[96,2048]{1,0:T(8,128)(2,1)S(1)} %collective-permute-done.151.rest_1_, ...), custom_call_target="tpu_custom_call" | custom-call | flops 4831838208 | bytes 12582912 | tf_op jit(solution)/shard_map/cond/branch_2_fun/pallas_call | solution.py:664
  231.6 3.7 collective-permute-start.161
  235.3 5.0 %collective-permute-done.157 = bf16[96,2048]{1,0:T(8,128)(2,1)S(1)} collective-permute-done((bf16[96,2048]{1,0:T(8,128)(2,1)S(1)}, bf16[96,2048]{1,0:T(8,128)(2,1)S(1)}, u32[]{:S(2)}, u32[]{:S(2)}) %collective-permute-start.157) | collective-permute-done | bytes 393248 | tf_op jit(solution)/shard_map/cond/branch_2_fun/ppermute | solution.py:470
  241.1 5.0 %collective-permute-start.159 = (bf16[96,2048]{1,0:T(8,128)(2,1)S(1)}, bf16[96,2048]{1,0:T(8,128)(2,1)S(1)}, u32[]{:S(2)}, u32[]{:S(2)}) collective-permute-start(bf16[96,2048]{1,0:T(8,128)(2,1)S(1)} %get-tuple-element.490), channel_id=1, source_target_pairs={{0,1},{1,2},{4,5},{5,6},{8,9},{9,10},{12,13},{13,14},{16,17},{17,1... | collective-permute-start | bytes 1179656 | tf_op jit(solution)/shard_map/cond/branch_2_fun/ppermute | solution.py:488
  246.1 5.4 %collective-permute-done.161 = bf16[128,2048]{1,0:T(8,128)(2,1)S(1)} collective-permute-done((bf16[128,2048]{1,0:T(8,128)(2,1)S(1)}, bf16[128,2048]{1,0:T(8,128)(2,1)S(1)}, u32[]{:S(2)}, u32[]{:S(2)}) %collective-permute-start.161) | collective-permute-done | bytes 524320 | tf_op jit(solution)/shard_map/cond/branch_2_fun/ppermute | solution.py:488
  252.9 5.3 %collective-permute-start.165 = (bf16[128,2048]{1,0:T(8,128)(2,1)S(1)}, bf16[128,2048]{1,0:T(8,128)(2,1)S(1)}, u32[]{:S(2)}, u32[]{:S(2)}) collective-permute-start(bf16[128,2048]{1,0:T(8,128)(2,1)S(1)} %get-tuple-element.495), channel_id=1, source_target_pairs={{0,1},{1,2},{2,3},{4,5},{5,6},{6,7},{8,9},{9,10},{10,11},{12,13},{... | collective-permute-start | bytes 1572872 | tf_op jit(solution)/shard_map/cond/branch_2_fun/ppermute | solution.py:488
  260.0 3.1 collective-permute-done.166.rest_2_
  263.2 3.0 collective-permute-done.165.rest_1_
  268.8 5.1 %collective-permute-start.170 = (bf16[128,2048]{1,0:T(8,128)(2,1)S(1)}, bf16[128,2048]{1,0:T(8,128)(2,1)S(1)}, u32[]{:S(2)}, u32[]{:S(2)}) collective-permute-start(bf16[128,2048]{1,0:T(8,128)(2,1)S(1)} %get-tuple-element.509.own), channel_id=1, source_target_pairs={{0,1},{1,2},{2,3},{4,5},{5,6},{6,7},{8,9},{9,10},{10,11},{12,13},{... | collective-permute-start | bytes 1572872 | tf_op jit(solution)/shard_map/cond/branch_2_fun/ppermute | solution.py:497
  275.2 6.6 %collective-permute-start.163 = (bf16[96,2048]{1,0:T(8,128)(2,1)S(1)}, bf16[96,2048]{1,0:T(8,128)(2,1)S(1)}, u32[]{:S(2)}, u32[]{:S(2)}) collective-permute-start(bf16[96,2048]{1,0:T(8,128)(2,1)S(1)} %get-tuple-element.498), channel_id=1, source_target_pairs={{0,1},{1,2},{2,3},{4,5},{5,6},{6,7},{8,9},{9,10},{10,11},{12,13},{... | collective-permute-start | bytes 1179656 | tf_op jit(solution)/shard_map/cond/branch_2_fun/ppermute | solution.py:488
  281.8 5.7 %collective-permute-done.164.rest_2_ = bf16[96,2048]{1,0:T(8,128)(2,1)S(1)} collective-permute-done((bf16[96,2048]{1,0:T(8,128)(2,1)S(1)}, bf16[96,2048]{1,0:T(8,128)(2,1)S(1)}, u32[]{:S(2)}, u32[]{:S(2)}) %collective-permute-start.164) | collective-permute-done | bytes 393248 | tf_op jit(solution)/shard_map/cond/branch_2_fun/ppermute | solution.py:489
  293.4 10.3 %collective-permute-start.167 = (bf16[96,2048]{1,0:T(8,128)(2,1)S(1)}, bf16[96,2048]{1,0:T(8,128)(2,1)S(1)}, u32[]{:S(2)}, u32[]{:S(2)}) collective-permute-start(bf16[96,2048]{1,0:T(8,128)(2,1)S(1)} %get-tuple-element.506.own), channel_id=1, source_target_pairs={{0,1},{1,2},{2,3},{4,5},{5,6},{6,7},{8,9},{9,10},{10,11},{12,13},{... | collective-permute-start | bytes 1179656 | tf_op jit(solution)/shard_map/cond/branch_2_fun/ppermute | solution.py:497
  305.3 2.7 collective-permute-done.169
  313.8 6.8 %collective-permute-start.179 = (bf16[16,2048]{1,0:T(8,128)(2,1)S(1)}, bf16[16,2048]{1,0:T(8,128)(2,1)S(1)}, u32[]{:S(2)}, u32[]{:S(2)}) collective-permute-start(bf16[16,2048]{1,0:T(8,128)(2,1)S(1)} %add.502), channel_id=1, source_target_pairs={{0,1},{1,0},{2,3},{3,2},{4,5},{5,4},{6,7},{7,6},{8,9},{9,8},{10,11... | collective-permute-start | bytes 196616 | tf_op jit(solution)/shard_map/cond/branch_2_fun/ppermute | solution.py:710
  322.1 5.1 %collective-permute-done.173.rest_4_ = bf16[96,2048]{1,0:T(8,128)(2,1)S(1)} collective-permute-done((bf16[96,2048]{1,0:T(8,128)(2,1)S(1)}, bf16[96,2048]{1,0:T(8,128)(2,1)S(1)}, u32[]{:S(2)}, u32[]{:S(2)}) %collective-permute-start.173) | collective-permute-done | bytes 393248 | tf_op jit(solution)/shard_map/cond/branch_2_fun/ppermute | solution.py:498
  328.6 6.2 %collective-permute-start.180 = (bf16[16,2048]{1,0:T(8,128)(2,1)S(1)}, bf16[16,2048]{1,0:T(8,128)(2,1)S(1)}, u32[]{:S(2)}, u32[]{:S(2)}) collective-permute-start(bf16[16,2048]{1,0:T(8,128)(2,1)S(1)} %add.503), channel_id=1, source_target_pairs={{0,2},{1,3},{2,0},{3,1},{4,6},{5,7},{6,4},{7,5},{8,10},{9,11},{10,... | collective-permute-start | bytes 196616 | tf_op jit(solution)/shard_map/cond/branch_2_fun/ppermute | solution.py:710
  337.1 2.7 collective-permute-done.178.rest_2_.rest_5_
  341.3 3.7 collective-permute-done.183
  345.0 2.7 branch_2_fun.37
  356.8 3.6 collective-permute-done.186
  361.8 3.2 collective-permute-done.187
  (204 shorter events, 96.1 us)
Async XLA Ops:
  15.6 187.0 %all-gather.13.cloned.1.call-start = ((), (), s32[]{:S(2)}) async-start(), calls=%async_computation.2 | async-start | bytes 14155776 | tf_op jit(solution)/shard_map/cond/branch_2_fun/all_gather | solution.py:622
  15.7 15.4 %collective-permute-start.126 = (bf16[2,16,2560]{2,1,0:T(8,128)(2,1)S(1)}, bf16[2,16,2560]{2,1,0:T(8,128)(2,1)S(1)}, u32[]{:S(2)}, u32[]{:S(2)}) collective-permute-start(bf16[2,16,2560]{2,1,0:T(8,128)(2,1)S(1)} %get-tuple-element.430), channel_id=1, source_target_pairs={{0,4},{4,0},{8,12},{12,8},{16,20},{20,16},{24,28},{28,24},{1,5},{5... | collective-permute-start | bytes 491528 | tf_op jit(solution)/shard_map/cond/branch_2_fun/ppermute | solution.py:529
  16.2 17.5 %collective-permute-start.127 = (bf16[2,16,2560]{2,1,0:T(8,128)(2,1)S(1)}, bf16[2,16,2560]{2,1,0:T(8,128)(2,1)S(1)}, u32[]{:S(2)}, u32[]{:S(2)}) collective-permute-start(bf16[2,16,2560]{2,1,0:T(8,128)(2,1)S(1)} %get-tuple-element.431), channel_id=1, source_target_pairs={{0,8},{4,12},{8,0},{12,4},{16,24},{20,28},{24,16},{28,20},{1,9},{5... | collective-permute-start | bytes 491528 | tf_op jit(solution)/shard_map/cond/branch_2_fun/ppermute | solution.py:529
  18.8 19.5 %collective-permute-start.128 = (bf16[2,16,2560]{2,1,0:T(8,128)(2,1)}, bf16[2,16,2560]{2,1,0:T(8,128)(2,1)S(1)}, u32[]{:S(2)}, u32[]{:S(2)}) collective-permute-start(bf16[2,16,2560]{2,1,0:T(8,128)(2,1)} %get-tuple-element.432), channel_id=1, source_target_pairs={{0,12},{4,8},{8,4},{12,0},{16,28},{20,24},{24,20},{28,16},{1,13},{... | collective-permute-start | bytes 491528 | tf_op jit(solution)/shard_map/cond/branch_2_fun/ppermute | solution.py:529
  18.8 19.4 %collective-permute-start.129 = (bf16[2,16,2560]{2,1,0:T(8,128)(2,1)}, bf16[2,16,2560]{2,1,0:T(8,128)(2,1)S(1)}, u32[]{:S(2)}, u32[]{:S(2)}) collective-permute-start(bf16[2,16,2560]{2,1,0:T(8,128)(2,1)} %get-tuple-element.433), channel_id=1, source_target_pairs={{0,16},{4,20},{8,24},{12,28},{16,0},{20,4},{24,8},{28,12},{1,17},{... | collective-permute-start | bytes 491528 | tf_op jit(solution)/shard_map/cond/branch_2_fun/ppermute | solution.py:529
  20.6 17.7 %collective-permute-start.130 = (bf16[2,16,2560]{2,1,0:T(8,128)(2,1)}, bf16[2,16,2560]{2,1,0:T(8,128)(2,1)S(1)}, u32[]{:S(2)}, u32[]{:S(2)}) collective-permute-start(bf16[2,16,2560]{2,1,0:T(8,128)(2,1)} %get-tuple-element.434), channel_id=1, source_target_pairs={{0,20},{4,16},{8,28},{12,24},{16,4},{20,0},{24,12},{28,8},{1,21},{... | collective-permute-start | bytes 491528 | tf_op jit(solution)/shard_map/cond/branch_2_fun/ppermute | solution.py:529
  69.4 16.2 %collective-permute-start.137 = (bf16[128,2048]{1,0:T(8,128)(2,1)}, bf16[128,2048]{1,0:T(8,128)(2,1)S(1)}, u32[]{:S(2)}, u32[]{:S(2)}) collective-permute-start(bf16[128,2048]{1,0:T(8,128)(2,1)} %get-tuple-element.747), channel_id=1, source_target_pairs={{0,1},{3,2},{4,5},{7,6},{8,9},{11,10},{12,13},{15,14},{16,17},{19,... | collective-permute-start | bytes 1572872 | tf_op jit(solution)/shard_map/cond/branch_2_fun/ppermute | solution.py:470
  79.2 15.6 %collective-permute-start.136 = (bf16[96,2048]{1,0:T(8,128)(2,1)S(1)}, bf16[96,2048]{1,0:T(8,128)(2,1)S(1)}, u32[]{:S(2)}, u32[]{:S(2)}) collective-permute-start(bf16[96,2048]{1,0:T(8,128)(2,1)S(1)} %get-tuple-element.448), channel_id=1, source_target_pairs={{0,1},{3,2},{4,5},{7,6},{8,9},{11,10},{12,13},{15,14},{16,17},{19,... | collective-permute-start | bytes 1179656 | tf_op jit(solution)/shard_map/cond/branch_2_fun/ppermute | solution.py:470
  85.7 15.1 %collective-permute-start.141 = (bf16[128,2048]{1,0:T(8,128)(2,1)S(1)}, bf16[128,2048]{1,0:T(8,128)(2,1)S(1)}, u32[]{:S(2)}, u32[]{:S(2)}) collective-permute-start(bf16[128,2048]{1,0:T(8,128)(2,1)S(1)} %get-tuple-element.456), channel_id=1, source_target_pairs={{3,2},{2,1},{7,6},{6,5},{11,10},{10,9},{15,14},{14,13},{19,18},{18... | collective-permute-start | bytes 1572872 | tf_op jit(solution)/shard_map/cond/branch_2_fun/ppermute | solution.py:489
  86.4 18.8 %collective-permute-start.140 = (bf16[128,2048]{1,0:T(8,128)(2,1)S(1)}, bf16[128,2048]{1,0:T(8,128)(2,1)S(1)}, u32[]{:S(2)}, u32[]{:S(2)}) collective-permute-start(bf16[128,2048]{1,0:T(8,128)(2,1)S(1)} %get-tuple-element.451), channel_id=1, source_target_pairs={{0,1},{1,2},{4,5},{5,6},{8,9},{9,10},{12,13},{13,14},{16,17},{17,1... | collective-permute-start | bytes 1572872 | tf_op jit(solution)/shard_map/cond/branch_2_fun/ppermute | solution.py:488
  94.7 19.0 %collective-permute-start.144 = (bf16[128,2048]{1,0:T(8,128)(2,1)S(1)}, bf16[128,2048]{1,0:T(8,128)(2,1)S(1)}, u32[]{:S(2)}, u32[]{:S(2)}) collective-permute-start(bf16[128,2048]{1,0:T(8,128)(2,1)S(1)} %get-tuple-element.468), channel_id=1, source_target_pairs={{0,4},{4,0},{8,12},{12,8},{16,20},{20,16},{24,28},{28,24},{1,5},{5... | collective-permute-start | bytes 1572872 | tf_op jit(solution)/shard_map/cond/branch_2_fun/ppermute | solution.py:635
  94.9 16.8 %collective-permute-start.139 = (bf16[96,2048]{1,0:T(8,128)(2,1)S(1)}, bf16[96,2048]{1,0:T(8,128)(2,1)S(1)}, u32[]{:S(2)}, u32[]{:S(2)}) collective-permute-start(bf16[96,2048]{1,0:T(8,128)(2,1)S(1)} %get-tuple-element.455), channel_id=1, source_target_pairs={{3,2},{2,1},{7,6},{6,5},{11,10},{10,9},{15,14},{14,13},{19,18},{18... | collective-permute-start | bytes 1179656 | tf_op jit(solution)/shard_map/cond/branch_2_fun/ppermute | solution.py:489
  95.7 17.9 %collective-permute-start.138 = (bf16[96,2048]{1,0:T(8,128)(2,1)S(1)}, bf16[96,2048]{1,0:T(8,128)(2,1)S(1)}, u32[]{:S(2)}, u32[]{:S(2)}) collective-permute-start(bf16[96,2048]{1,0:T(8,128)(2,1)S(1)} %get-tuple-element.454), channel_id=1, source_target_pairs={{0,1},{1,2},{4,5},{5,6},{8,9},{9,10},{12,13},{13,14},{16,17},{17,1... | collective-permute-start | bytes 1179656 | tf_op jit(solution)/shard_map/cond/branch_2_fun/ppermute | solution.py:488
  105.3 15.3 %collective-permute-start.146 = (bf16[128,2048]{1,0:T(8,128)(2,1)S(1)}, bf16[128,2048]{1,0:T(8,128)(2,1)S(1)}, u32[]{:S(2)}, u32[]{:S(2)}) collective-permute-start(bf16[128,2048]{1,0:T(8,128)(2,1)S(1)} %get-tuple-element.469), channel_id=1, source_target_pairs={{3,2},{2,1},{1,0},{7,6},{6,5},{5,4},{11,10},{10,9},{9,8},{15,14},{... | collective-permute-start | bytes 1572872 | tf_op jit(solution)/shard_map/cond/branch_2_fun/ppermute | solution.py:489
  106.6 17.5 %collective-permute-start.145 = (bf16[128,2048]{1,0:T(8,128)(2,1)S(1)}, bf16[128,2048]{1,0:T(8,128)(2,1)S(1)}, u32[]{:S(2)}, u32[]{:S(2)}) collective-permute-start(bf16[128,2048]{1,0:T(8,128)(2,1)S(1)} %get-tuple-element.459), channel_id=1, source_target_pairs={{0,1},{1,2},{2,3},{4,5},{5,6},{6,7},{8,9},{9,10},{10,11},{12,13},{... | collective-permute-start | bytes 1572872 | tf_op jit(solution)/shard_map/cond/branch_2_fun/ppermute | solution.py:488
  125.2 26.6 %collective-permute-start.150 = (bf16[128,2048]{1,0:T(8,128)(2,1)S(1)}, bf16[128,2048]{1,0:T(8,128)(2,1)}, u32[]{:S(2)}, u32[]{:S(2)}) collective-permute-start(bf16[128,2048]{1,0:T(8,128)(2,1)S(1)} %get-tuple-element.474.own), channel_id=1, source_target_pairs={{1,0},{2,1},{3,2},{5,4},{6,5},{7,6},{9,8},{10,9},{11,10},{13,12},{... | collective-permute-start | bytes 1572872 | tf_op jit(solution)/shard_map/cond/branch_2_fun/ppermute | solution.py:498
  126.5 25.3 %collective-permute-start.149 = (bf16[128,2048]{1,0:T(8,128)(2,1)S(1)}, bf16[128,2048]{1,0:T(8,128)(2,1)}, u32[]{:S(2)}, u32[]{:S(2)}) collective-permute-start(bf16[128,2048]{1,0:T(8,128)(2,1)S(1)} %get-tuple-element.474.own), channel_id=1, source_target_pairs={{0,1},{1,2},{2,3},{4,5},{5,6},{6,7},{8,9},{9,10},{10,11},{12,13},{... | collective-permute-start | bytes 1572872 | tf_op jit(solution)/shard_map/cond/branch_2_fun/ppermute | solution.py:497
  132.4 17.3 %collective-permute-start.143 = (bf16[96,2048]{1,0:T(8,128)(2,1)S(1)}, bf16[96,2048]{1,0:T(8,128)(2,1)S(1)}, u32[]{:S(2)}, u32[]{:S(2)}) collective-permute-start(bf16[96,2048]{1,0:T(8,128)(2,1)S(1)} %get-tuple-element.463), channel_id=1, source_target_pairs={{3,2},{2,1},{1,0},{7,6},{6,5},{5,4},{11,10},{10,9},{9,8},{15,14},{... | collective-permute-start | bytes 1179656 | tf_op jit(solution)/shard_map/cond/branch_2_fun/ppermute | solution.py:489
  133.7 17.1 %collective-permute-start.142 = (bf16[96,2048]{1,0:T(8,128)(2,1)S(1)}, bf16[96,2048]{1,0:T(8,128)(2,1)S(1)}, u32[]{:S(2)}, u32[]{:S(2)}) collective-permute-start(bf16[96,2048]{1,0:T(8,128)(2,1)S(1)} %get-tuple-element.462), channel_id=1, source_target_pairs={{0,1},{1,2},{2,3},{4,5},{5,6},{6,7},{8,9},{9,10},{10,11},{12,13},{... | collective-permute-start | bytes 1179656 | tf_op jit(solution)/shard_map/cond/branch_2_fun/ppermute | solution.py:488
  151.8 25.8 %collective-permute-start.154 = (bf16[128,2048]{1,0:T(8,128)(2,1)}, bf16[128,2048]{1,0:T(8,128)(2,1)S(1)}, u32[]{:S(2)}, u32[]{:S(2)}) collective-permute-start(bf16[128,2048]{1,0:T(8,128)(2,1)} %collective-permute-done.150.rest_3_), channel_id=1, source_target_pairs={{1,0},{2,1},{5,4},{6,5},{9,8},{10,9},{13,12},{14,13},{17,16},{18,1... | collective-permute-start | bytes 1572872 | tf_op jit(solution)/shard_map/cond/branch_2_fun/ppermute | solution.py:498
  153.1 24.5 %collective-permute-start.153 = (bf16[128,2048]{1,0:T(8,128)(2,1)}, bf16[128,2048]{1,0:T(8,128)(2,1)S(1)}, u32[]{:S(2)}, u32[]{:S(2)}) collective-permute-start(bf16[128,2048]{1,0:T(8,128)(2,1)} %collective-permute-done.149.rest_0_), channel_id=1, source_target_pairs={{1,2},{2,3},{5,6},{6,7},{9,10},{10,11},{13,14},{14,15},{17,18},{18... | collective-permute-start | bytes 1572872 | tf_op jit(solution)/shard_map/cond/branch_2_fun/ppermute | solution.py:497
  153.8 21.8 %collective-permute-start.148 = (bf16[96,2048]{1,0:T(8,128)(2,1)S(1)}, bf16[96,2048]{1,0:T(8,128)(2,1)}, u32[]{:S(2)}, u32[]{:S(2)}) collective-permute-start(bf16[96,2048]{1,0:T(8,128)(2,1)S(1)} %get-tuple-element.473.own), channel_id=1, source_target_pairs={{1,0},{2,1},{3,2},{5,4},{6,5},{7,6},{9,8},{10,9},{11,10},{13,12},{... | collective-permute-start | bytes 1179656 | tf_op jit(solution)/shard_map/cond/branch_2_fun/ppermute | solution.py:498
  155.1 20.5 %collective-permute-start.147 = (bf16[96,2048]{1,0:T(8,128)(2,1)S(1)}, bf16[96,2048]{1,0:T(8,128)(2,1)}, u32[]{:S(2)}, u32[]{:S(2)}) collective-permute-start(bf16[96,2048]{1,0:T(8,128)(2,1)S(1)} %get-tuple-element.473.own), channel_id=1, source_target_pairs={{0,1},{1,2},{2,3},{4,5},{5,6},{6,7},{8,9},{9,10},{10,11},{12,13},{... | collective-permute-start | bytes 1179656 | tf_op jit(solution)/shard_map/cond/branch_2_fun/ppermute | solution.py:497
  175.6 15.0 %collective-permute-start.152 = (bf16[96,2048]{1,0:T(8,128)(2,1)}, bf16[96,2048]{1,0:T(8,128)(2,1)S(1)}, u32[]{:S(2)}, u32[]{:S(2)}) collective-permute-start(bf16[96,2048]{1,0:T(8,128)(2,1)} %collective-permute-done.148.rest_3_), channel_id=1, source_target_pairs={{1,0},{2,1},{5,4},{6,5},{9,8},{10,9},{13,12},{14,13},{17,16},{18,1... | collective-permute-start | bytes 1179656 | tf_op jit(solution)/shard_map/cond/branch_2_fun/ppermute | solution.py:498
  176.9 13.7 %collective-permute-start.151 = (bf16[96,2048]{1,0:T(8,128)(2,1)}, bf16[96,2048]{1,0:T(8,128)(2,1)S(1)}, u32[]{:S(2)}, u32[]{:S(2)}) collective-permute-start(bf16[96,2048]{1,0:T(8,128)(2,1)} %collective-permute-done.147.rest_0_), channel_id=1, source_target_pairs={{1,2},{2,3},{5,6},{6,7},{9,10},{10,11},{13,14},{14,15},{17,18},{18... | collective-permute-start | bytes 1179656 | tf_op jit(solution)/shard_map/cond/branch_2_fun/ppermute | solution.py:497
  177.7 24.1 %collective-permute-start.156 = (bf16[128,2048]{1,0:T(8,128)(2,1)S(1)}, bf16[128,2048]{1,0:T(8,128)(2,1)S(1)}, u32[]{:S(2)}, u32[]{:S(2)}) collective-permute-start(bf16[128,2048]{1,0:T(8,128)(2,1)S(1)} %broadcast_select_fusion.9), channel_id=1, source_target_pairs={{2,3},{1,0},{6,7},{5,4},{10,11},{9,8},{14,15},{13,12},{18,19},{17,... | collective-permute-start | bytes 1572872 | tf_op jit(solution)/shard_map/cond/branch_2_fun/ppermute | solution.py:501
  191.5 28.8 %collective-permute-start.155 = (bf16[96,2048]{1,0:T(8,128)(2,1)}, bf16[96,2048]{1,0:T(8,128)(2,1)}, u32[]{:S(2)}, u32[]{:S(2)}) collective-permute-start(bf16[96,2048]{1,0:T(8,128)(2,1)} %broadcast_select_fusion.11), channel_id=1, source_target_pairs={{2,3},{1,0},{6,7},{5,4},{10,11},{9,8},{14,15},{13,12},{18,19},{17,... | collective-permute-start | bytes 1179656 | tf_op jit(solution)/shard_map/cond/branch_2_fun/ppermute | solution.py:501
  218.6 12.1 %collective-permute-start.158 = (bf16[128,2048]{1,0:T(8,128)(2,1)S(1)}, bf16[128,2048]{1,0:T(8,128)(2,1)S(1)}, u32[]{:S(2)}, u32[]{:S(2)}) collective-permute-start(bf16[128,2048]{1,0:T(8,128)(2,1)S(1)} %get-tuple-element.483), channel_id=1, source_target_pairs={{0,1},{3,2},{4,5},{7,6},{8,9},{11,10},{12,13},{15,14},{16,17},{19,... | collective-permute-start | bytes 1572872 | tf_op jit(solution)/shard_map/cond/branch_2_fun/ppermute | solution.py:470
  230.9 15.2 %collective-permute-start.162 = (bf16[128,2048]{1,0:T(8,128)(2,1)S(1)}, bf16[128,2048]{1,0:T(8,128)(2,1)S(1)}, u32[]{:S(2)}, u32[]{:S(2)}) collective-permute-start(bf16[128,2048]{1,0:T(8,128)(2,1)S(1)} %get-tuple-element.492), channel_id=1, source_target_pairs={{3,2},{2,1},{7,6},{6,5},{11,10},{10,9},{15,14},{14,13},{19,18},{18... | collective-permute-start | bytes 1572872 | tf_op jit(solution)/shard_map/cond/branch_2_fun/ppermute | solution.py:489
  231.6 19.9 %collective-permute-start.161 = (bf16[128,2048]{1,0:T(8,128)(2,1)S(1)}, bf16[128,2048]{1,0:T(8,128)(2,1)S(1)}, u32[]{:S(2)}, u32[]{:S(2)}) collective-permute-start(bf16[128,2048]{1,0:T(8,128)(2,1)S(1)} %get-tuple-element.487), channel_id=1, source_target_pairs={{0,1},{1,2},{4,5},{5,6},{8,9},{9,10},{12,13},{13,14},{16,17},{17,1... | collective-permute-start | bytes 1572872 | tf_op jit(solution)/shard_map/cond/branch_2_fun/ppermute | solution.py:488
  240.4 17.8 %collective-permute-start.160 = (bf16[96,2048]{1,0:T(8,128)(2,1)S(1)}, bf16[96,2048]{1,0:T(8,128)(2,1)S(1)}, u32[]{:S(2)}, u32[]{:S(2)}) collective-permute-start(bf16[96,2048]{1,0:T(8,128)(2,1)S(1)} %get-tuple-element.491), channel_id=1, source_target_pairs={{3,2},{2,1},{7,6},{6,5},{11,10},{10,9},{15,14},{14,13},{19,18},{18... | collective-permute-start | bytes 1179656 | tf_op jit(solution)/shard_map/cond/branch_2_fun/ppermute | solution.py:489
  241.1 18.9 %collective-permute-start.159 = (bf16[96,2048]{1,0:T(8,128)(2,1)S(1)}, bf16[96,2048]{1,0:T(8,128)(2,1)S(1)}, u32[]{:S(2)}, u32[]{:S(2)}) collective-permute-start(bf16[96,2048]{1,0:T(8,128)(2,1)S(1)} %get-tuple-element.490), channel_id=1, source_target_pairs={{0,1},{1,2},{4,5},{5,6},{8,9},{9,10},{12,13},{13,14},{16,17},{17,1... | collective-permute-start | bytes 1179656 | tf_op jit(solution)/shard_map/cond/branch_2_fun/ppermute | solution.py:488
  252.9 13.3 %collective-permute-start.165 = (bf16[128,2048]{1,0:T(8,128)(2,1)S(1)}, bf16[128,2048]{1,0:T(8,128)(2,1)S(1)}, u32[]{:S(2)}, u32[]{:S(2)}) collective-permute-start(bf16[128,2048]{1,0:T(8,128)(2,1)S(1)} %get-tuple-element.495), channel_id=1, source_target_pairs={{0,1},{1,2},{2,3},{4,5},{5,6},{6,7},{8,9},{9,10},{10,11},{12,13},{... | collective-permute-start | bytes 1572872 | tf_op jit(solution)/shard_map/cond/branch_2_fun/ppermute | solution.py:488
  267.3 22.8 %collective-permute-start.171 = (bf16[128,2048]{1,0:T(8,128)(2,1)S(1)}, bf16[128,2048]{1,0:T(8,128)(2,1)S(1)}, u32[]{:S(2)}, u32[]{:S(2)}) collective-permute-start(bf16[128,2048]{1,0:T(8,128)(2,1)S(1)} %get-tuple-element.509.own), channel_id=1, source_target_pairs={{1,0},{2,1},{3,2},{5,4},{6,5},{7,6},{9,8},{10,9},{11,10},{13,12},{... | collective-permute-start | bytes 1572872 | tf_op jit(solution)/shard_map/cond/branch_2_fun/ppermute | solution.py:498
  268.8 21.4 %collective-permute-start.170 = (bf16[128,2048]{1,0:T(8,128)(2,1)S(1)}, bf16[128,2048]{1,0:T(8,128)(2,1)S(1)}, u32[]{:S(2)}, u32[]{:S(2)}) collective-permute-start(bf16[128,2048]{1,0:T(8,128)(2,1)S(1)} %get-tuple-element.509.own), channel_id=1, source_target_pairs={{0,1},{1,2},{2,3},{4,5},{5,6},{6,7},{8,9},{9,10},{10,11},{12,13},{... | collective-permute-start | bytes 1572872 | tf_op jit(solution)/shard_map/cond/branch_2_fun/ppermute | solution.py:497
  273.9 13.6 %collective-permute-start.164 = (bf16[96,2048]{1,0:T(8,128)(2,1)S(1)}, bf16[96,2048]{1,0:T(8,128)(2,1)S(1)}, u32[]{:S(2)}, u32[]{:S(2)}) collective-permute-start(bf16[96,2048]{1,0:T(8,128)(2,1)S(1)} %get-tuple-element.499), channel_id=1, source_target_pairs={{3,2},{2,1},{1,0},{7,6},{6,5},{5,4},{11,10},{10,9},{9,8},{15,14},{... | collective-permute-start | bytes 1179656 | tf_op jit(solution)/shard_map/cond/branch_2_fun/ppermute | solution.py:489
  275.2 13.8 %collective-permute-start.163 = (bf16[96,2048]{1,0:T(8,128)(2,1)S(1)}, bf16[96,2048]{1,0:T(8,128)(2,1)S(1)}, u32[]{:S(2)}, u32[]{:S(2)}) collective-permute-start(bf16[96,2048]{1,0:T(8,128)(2,1)S(1)} %get-tuple-element.498), channel_id=1, source_target_pairs={{0,1},{1,2},{2,3},{4,5},{5,6},{6,7},{8,9},{9,10},{10,11},{12,13},{... | collective-permute-start | bytes 1179656 | tf_op jit(solution)/shard_map/cond/branch_2_fun/ppermute | solution.py:488
  290.1 30.5 %collective-permute-start.175 = (bf16[128,2048]{1,0:T(8,128)(2,1)S(1)}, bf16[128,2048]{1,0:T(8,128)(2,1)S(1)}, u32[]{:S(2)}, u32[]{:S(2)}) collective-permute-start(bf16[128,2048]{1,0:T(8,128)(2,1)S(1)} %collective-permute-done.171.rest_3_), channel_id=1, source_target_pairs={{1,0},{2,1},{5,4},{6,5},{9,8},{10,9},{13,12},{14,13},{17,16},{18,1... | collective-permute-start | bytes 1572872 | tf_op jit(solution)/shard_map/cond/branch_2_fun/ppermute | solution.py:498
  291.4 29.2 %collective-permute-start.174 = (bf16[128,2048]{1,0:T(8,128)(2,1)S(1)}, bf16[128,2048]{1,0:T(8,128)(2,1)S(1)}, u32[]{:S(2)}, u32[]{:S(2)}) collective-permute-start(bf16[128,2048]{1,0:T(8,128)(2,1)S(1)} %collective-permute-done.170.rest_0_), channel_id=1, source_target_pairs={{1,2},{2,3},{5,6},{6,7},{9,10},{10,11},{13,14},{14,15},{17,18},{18... | collective-permute-start | bytes 1572872 | tf_op jit(solution)/shard_map/cond/branch_2_fun/ppermute | solution.py:497
  292.1 19.7 %collective-permute-start.168 = (bf16[96,2048]{1,0:T(8,128)(2,1)S(1)}, bf16[96,2048]{1,0:T(8,128)(2,1)S(1)}, u32[]{:S(2)}, u32[]{:S(2)}) collective-permute-start(bf16[96,2048]{1,0:T(8,128)(2,1)S(1)} %get-tuple-element.506.own), channel_id=1, source_target_pairs={{1,0},{2,1},{3,2},{5,4},{6,5},{7,6},{9,8},{10,9},{11,10},{13,12},{... | collective-permute-start | bytes 1179656 | tf_op jit(solution)/shard_map/cond/branch_2_fun/ppermute | solution.py:498
  293.4 18.4 %collective-permute-start.167 = (bf16[96,2048]{1,0:T(8,128)(2,1)S(1)}, bf16[96,2048]{1,0:T(8,128)(2,1)S(1)}, u32[]{:S(2)}, u32[]{:S(2)}) collective-permute-start(bf16[96,2048]{1,0:T(8,128)(2,1)S(1)} %get-tuple-element.506.own), channel_id=1, source_target_pairs={{0,1},{1,2},{2,3},{4,5},{5,6},{6,7},{8,9},{9,10},{10,11},{12,13},{... | collective-permute-start | bytes 1179656 | tf_op jit(solution)/shard_map/cond/branch_2_fun/ppermute | solution.py:497
  311.8 15.4 %collective-permute-start.173 = (bf16[96,2048]{1,0:T(8,128)(2,1)S(1)}, bf16[96,2048]{1,0:T(8,128)(2,1)S(1)}, u32[]{:S(2)}, u32[]{:S(2)}) collective-permute-start(bf16[96,2048]{1,0:T(8,128)(2,1)S(1)} %collective-permute-done.168.rest_3_), channel_id=1, source_target_pairs={{1,0},{2,1},{5,4},{6,5},{9,8},{10,9},{13,12},{14,13},{17,16},{18,1... | collective-permute-start | bytes 1179656 | tf_op jit(solution)/shard_map/cond/branch_2_fun/ppermute | solution.py:498
  313.1 14.1 %collective-permute-start.172 = (bf16[96,2048]{1,0:T(8,128)(2,1)S(1)}, bf16[96,2048]{1,0:T(8,128)(2,1)S(1)}, u32[]{:S(2)}, u32[]{:S(2)}) collective-permute-start(bf16[96,2048]{1,0:T(8,128)(2,1)S(1)} %collective-permute-done.167.rest_0_), channel_id=1, source_target_pairs={{1,2},{2,3},{5,6},{6,7},{9,10},{10,11},{13,14},{14,15},{17,18},{18... | collective-permute-start | bytes 1179656 | tf_op jit(solution)/shard_map/cond/branch_2_fun/ppermute | solution.py:497
  313.8 14.8 %collective-permute-start.179 = (bf16[16,2048]{1,0:T(8,128)(2,1)S(1)}, bf16[16,2048]{1,0:T(8,128)(2,1)S(1)}, u32[]{:S(2)}, u32[]{:S(2)}) collective-permute-start(bf16[16,2048]{1,0:T(8,128)(2,1)S(1)} %add.502), channel_id=1, source_target_pairs={{0,1},{1,0},{2,3},{3,2},{4,5},{5,4},{6,7},{7,6},{8,9},{9,8},{10,11... | collective-permute-start | bytes 196616 | tf_op jit(solution)/shard_map/cond/branch_2_fun/ppermute | solution.py:710
  320.7 19.1 %collective-permute-start.178 = (bf16[128,2048]{1,0:T(8,128)(2,1)S(1)}, bf16[128,2048]{1,0:T(8,128)(2,1)S(1)}, u32[]{:S(2)}, u32[]{:S(2)}) collective-permute-start(bf16[128,2048]{1,0:T(8,128)(2,1)S(1)} %broadcast_select_fusion.8), channel_id=1, source_target_pairs={{2,3},{1,0},{6,7},{5,4},{10,11},{9,8},{14,15},{13,12},{18,19},{17,... | collective-permute-start | bytes 1572872 | tf_op jit(solution)/shard_map/cond/branch_2_fun/ppermute | solution.py:501
  327.2 20.5 %collective-permute-start.177 = (bf16[96,2048]{1,0:T(8,128)(2,1)S(1)}, bf16[96,2048]{1,0:T(8,128)(2,1)S(1)}, u32[]{:S(2)}, u32[]{:S(2)}) collective-permute-start(bf16[96,2048]{1,0:T(8,128)(2,1)S(1)} %broadcast_select_fusion.10), channel_id=1, source_target_pairs={{2,3},{1,0},{6,7},{5,4},{10,11},{9,8},{14,15},{13,12},{18,19},{17,... | collective-permute-start | bytes 1179656 | tf_op jit(solution)/shard_map/cond/branch_2_fun/ppermute | solution.py:501
  340.7 26.9 %collective-permute-start.182 = (bf16[512,2048]{1,0:T(8,128)(2,1)S(1)}, bf16[512,2048]{1,0:T(8,128)(2,1)S(1)}, u32[]{:S(2)}, u32[]{:S(2)}) collective-permute-start(bf16[512,2048]{1,0:T(8,128)(2,1)S(1)} %branch_2_fun.33.mine), channel_id=1, source_target_pairs={{0,4},{4,0},{8,12},{12,8},{16,20},{20,16},{24,28},{28,24},{1,5},{5... | collective-permute-start | bytes 6291464 | tf_op jit(solution)/shard_map/cond/branch_2_fun/ppermute | solution.py:739
  350.8 17.7 %collective-permute-start.181 = (bf16[384,2048]{1,0:T(8,128)(2,1)S(1)}, bf16[384,2048]{1,0:T(8,128)(2,1)S(1)}, u32[]{:S(2)}, u32[]{:S(2)}) collective-permute-start(bf16[384,2048]{1,0:T(8,128)(2,1)S(1)} %branch_2_fun.34.mine), channel_id=1, source_target_pairs={{0,4},{4,0},{8,12},{12,8},{16,20},{20,16},{24,28},{28,24},{1,5},{5... | collective-permute-start | bytes 4718600 | tf_op jit(solution)/shard_map/cond/branch_2_fun/ppermute | solution.py:739
  (50 other events, 448.3 us)
Sparse Core Ops, SparseCore 0:
  56.0 73.6 all-gather.12
where the time goes:
time: 388 us
  starting transfers between devices  136 us (35%)
  waiting for transfers between devices  126 us (32%)
  Pallas kernels  72.3 us (19%)
  local copies, waits for them, and re-layouts  19.7 us (5%)
  loops' own time  15.3 us (4%)
  between operations  15.3 us (4%)
    ppermute x8, starting transfers between devices, reduce_step(): lax.ppermute(right, 'mlp', [(i, i + 1) for i in range(s)])  40.4 us
    ppermute x8, starting transfers between devices, spread_step(): lax.ppermute(right, 'mlp', [(i, i + 1) for i in range(s - 1, last)])  33.7 us
    ppermute x8, waiting for transfers between devices, spread_step(): lax.ppermute(left, 'mlp', [(i + 1, i) for i in range(0, nz - s)])  28.9 us
    ppermute x8, waiting for transfers between devices, reduce_step(): lax.ppermute(left, 'mlp', [(last - i, last - 1 - i) for i in range(s)])  27.1 us
    ppermute x8, waiting for transfers between devices, reduce_step(): lax.ppermute(right, 'mlp', [(i, i + 1) for i in range(s)])  22.7 us
    pallas_call x2, Pallas kernels, layer(): call(functools.partial(unit_kernel, nz), (units // UNIT,), [ANY] * (2 * n...  19.4 us
    cond x68, local copies, waits for them, and re-layouts  17.8 us
    ppermute x5, starting transfers between devices, share(): every = every + lax.ppermute(message, *steps[step])  16.6 us
  transfers between devices with their start and end apart: 64, of which 32 were waited for; matrix products, arithmetic and copies ran while one was open for 1% of the time, Pallas kernels for 14%

commit v1 on v0

--- a/solution.py
+++ b/solution.py
@@ -34,7 +34,7 @@
 
 
 def call(
-    kernel, grid, ins, outs, shapes, scratch=(), flops=0, nbytes=0, aliases=None, vmem=16
+    kernel, grid, ins, outs, shapes, scratch=(), flops=0, nbytes=0, aliases=None, vmem=12
 ):
     spec = pltpu.PrefetchScalarGridSpec(
         num_scalar_prefetch=1, grid=grid, in_specs=ins, out_specs=outs, scratch_shapes=scratch
@@ -552,7 +552,7 @@
                     jax.ShapeDtypeStruct((part_rows, columns), F32),
                     jax.ShapeDtypeStruct((part_rows, width), BF16),
                 ],
-                vmem=32,
+                vmem=26,
                 flops=2 * part_rows * width * 3 * columns,
                 nbytes=2 * (2 * part_rows * width + 3 * width * columns),
             )(info, hidden, gain_attn, w_qkv, cosine, sine)
@@ -602,7 +602,7 @@
             [whole(w_out.shape)] + [whole((part_rows, columns))] * len(parts),
             whole(part_shape.shape),
             part_shape,
-            vmem=24,
+            vmem=18,
             flops=2 * size * columns * (2 * part_rows + width),
             nbytes=2 * (columns * (2 * part_rows + width) + size * width),
         )(info, w_out, *parts)
@@ -627,7 +627,7 @@
         [whole((rows, width))],
         quarter_specs * 2,
         quarter_shapes * 2,
-        vmem=20,
+        vmem=16,
         flops=4 * sum(quarters) * rows * width,
         nbytes=2 * rows * width,
     )(following(info, head_parts[0]), hidden.reshape(rows, width))
@@ -648,7 +648,13 @@
             [spec, spec],
             [quarter_shapes[h]] * 2,
             nbytes=14 * q * width,
-        )(following(info, head_parts[1]), hidden_own[h], hidden_other[h], gain_mlp, *terms)
+        )(
+            following(info, head_parts[1] if h == 0 else weights),
+            hidden_own[h],
+            hidden_other[h],
+            gain_mlp,
+            *terms,
+        )
         streams.append(stream)
         rights.append([mid])
         lefts.append([mid])
@@ -673,7 +679,7 @@
                 pltpu.VMEM((size, width), F32),
                 pltpu.SemaphoreType.DMA((nz,)),
             ],
-            vmem=28,
+            vmem=24,
             flops=6 * size * width * units,
             nbytes=2 * weights.size,
         )(info, *rights[h], *lefts[h][1:], weights)
@@ -826,7 +832,8 @@
     ]
     if len(branches) == 1:
         return branches[0](*operands)
-    return lax.switch(info[CLASS], branches, *operands)
+    index = (info[CLASS] + 1) % len(branches)
+    return lax.switch(index, branches[-1:] + branches[:-1], *operands)
 
 
 def solution(mesh):

time: 388 us -> 374 us (0.964)
  waiting for transfers between devices: 126 us -> 120 us
  starting transfers between devices: 136 us -> 131 us
    ppermute x5, starting transfers between devices: 16.6 us -> 5.63 us  [share(): every = every + lax.ppermute(message, *steps[step])]
    ppermute x8, waiting for transfers between devices: 22.7 us -> 12 us  [reduce_step(): lax.ppermute(right, 'mlp', [(i, i + 1) for i in range(s)])]
    ppermute x8, starting transfers between devices: 40.4 us -> 45.8 us  [reduce_step(): lax.ppermute(right, 'mlp', [(i, i + 1) for i in range(s)])]
    ppermute x5, waiting for transfers between devices: 8.88 us -> 13.4 us  [share(): every = every + lax.ppermute(message, *steps[step])]
    cond x68 -> x62, local copies, waits for them, and re-layouts: 17.8 us -> 15.2 us
  transfers between devices with their start and end apart: 64 -> 64, of which waited for: 32 -> 34; matrix products, arithmetic and copies ran while one was open for 1% -> 1% of each run, Pallas kernels for 14% -> 15%
where the time goes in v1:
time: 374 us; the launch traced here: 372 us
  starting transfers between devices  131 us (35%)
  waiting for transfers between devices  120 us (32%)
  Pallas kernels  71.3 us (19%)
  local copies, waits for them, and re-layouts  17.1 us (5%)
  between operations  14.9 us (4%)
  loops' own time  14.7 us (4%)
    ppermute x8, starting transfers between devices, reduce_step(): lax.ppermute(right, 'mlp', [(i, i + 1) for i in range(s)])  45.8 us
    ppermute x8, starting transfers between devices, spread_step(): lax.ppermute(right, 'mlp', [(i, i + 1) for i in range(s - 1, last)])  35 us
    ppermute x8, waiting for transfers between devices, spread_step(): lax.ppermute(left, 'mlp', [(i + 1, i) for i in range(0, nz - s)])  30.3 us
    ppermute x8, waiting for transfers between devices, reduce_step(): lax.ppermute(left, 'mlp', [(last - i, last - 1 - i) for i in range(s)])  27.4 us
    pallas_call x2, Pallas kernels, layer(): call(functools.partial(unit_kernel, nz), (units // UNIT,), [ANY] * (2 * n...  18.1 us
    cond x62, local copies, waits for them, and re-layouts  15.2 us
    another operation x1, loops' own time, per_device(): return lax.switch(index, branches[-1:] + branches[:-1], *operands)  14.7 us
    pallas_call x2, Pallas kernels, layer(): call(functools.partial(attend_kernel, slots, table_rows, n, h), (slots,),...  13.7 us
  transfers between devices with their start and end apart: 64, of which 34 were waited for; matrix products, arithmetic and copies ran while one was open for 1% of the time, Pallas kernels for 15%

profile of v1, /device:TPU:0, one launch (start us, length us, event | category | flops | bytes accessed | tf_op | source)
XLA Modules:
  0.0 371.9 jit_solution(9003453446820457424)
XLA Ops:
  10.3 354.5 %conditional.1 = (bf16[2,512,2048]{2,1,0:T(8,128)(2,1)}, f32[16]{0:T(128)}, f32[16]{0:T(128)}) conditional(s32[]{:T(128)} %clamp.3, (s32[26]{0:T(128)S(1)}, bf16[2,512,2048]{2,1,0:T(8,128)(2,1)}, f32[1,2048]{1,0:T(1,128)}, bf16[3,2048,512]{2,1,0:T(8,128)(2,1)}, f32[512,128]{1,0:T(8,128)}, ...), branch_computations={%region_0.3_spmd, %region_3.6_spmd, %region_6.9_spmd, %region_9.12... | conditional | flops 27556188160 | bytes 602890624 | solution.py:836
  16.0 2.6 collective-permute-start.127
  20.4 8.1 %branch_2_fun.19 = (bf16[512,512]{1,0:T(8,128)(2,1)S(1)}, bf16[512,512]{1,0:T(8,128)(2,1)S(1)}, f32[512,512]{1,0:T(8,128)S(1)}, bf16[512,2048]{1,0:T(8,128)(2,1)S(1)}) custom-call(s32[26]{0:T(128)S(1)} %get-tuple-element.471.info, bf16[2,512,2048]{2,1,0:T(8,128)(2,1)} %get-tuple-element.420.x_ref, f32[1,2048]{1,0:T(1,128)} %get-tuple-element.421.gain_ref, ...), custom_call_target="tpu_custom_call" | custom-call | flops 3221225472 | bytes 10485760 | tf_op jit(solution)/shard_map/cond/branch_2_fun/pallas_call | solution.py:538
  30.9 2.6 collective-permute-start.131
  33.6 4.4 %branch_2_fun.20 = (bf16[512,512]{1,0:T(8,128)(2,1)S(1)}, bf16[512,512]{1,0:T(8,128)(2,1)S(1)}, f32[512,512]{1,0:T(8,128)S(1)}, bf16[512,2048]{1,0:T(8,128)(2,1)S(1)}) custom-call(s32[26]{0:T(128)S(1)} %get-tuple-element.471.info, bf16[2,512,2048]{2,1,0:T(8,128)(2,1)S(1)} %copy-done.116, f32[1,2048]{1,0:T(1,128)S(1)} %copy-done.122, ...), custom_call_target="tpu_custom_call" | custom-call | flops 3221225472 | bytes 10485760 | tf_op jit(solution)/shard_map/cond/branch_2_fun/pallas_call | solution.py:538
  38.8 2.5 collective-permute-done.132.rest_9_
  41.2 5.8 %branch_2_fun.21 = (bf16[512,512]{1,0:T(8,128)(2,1)S(1)}, bf16[2,16,2560]{2,1,0:T(8,128)(2,1)S(1)}) custom-call(s32[26]{0:T(128)S(1)} %get-tuple-element.471.info, f32[512,512]{1,0:T(8,128)S(1)} %get-tuple-element.427.q_ref, bf16[512,2048]{1,0:T(8,128)(2,1)S(1)} %get-tuple-element.428.normed_ref, f32[512,128]{1,0:T(8,128)S(1)} %copy-done.83, ...), custom_call_target="tpu_custom_call" | custom-call | flops 536870912 | bytes 5242880 | tf_op jit(solution)/shard_map/cond/branch_2_fun/pallas_call | solution.py:570
  49.1 2.4 branch_2_fun.22
  51.5 3.9 %branch_2_fun.23 = bf16[4,768,256]{2,1,0:T(8,128)(2,1)} custom-call(s32[26]{0:T(128)S(1)} %get-tuple-element.471.info, bf16[256,2,1024]{2,1,0:T(2,128)(2,1)S(1)} %copy-done.87, bf16[1024,256]{1,0:T(8,128)(2,1)S(1)} %copy-done.91), custom_call_target="tpu_custom_call" | custom-call | bytes 3145728 | tf_op jit(solution)/shard_map/cond/branch_2_fun/pallas_call | solution.py:614
  60.7 7.9 %branch_2_fun.25.rest_0_ = bf16[512,512]{1,0:T(8,128)(2,1)} custom-call(s32[26]{0:T(128)S(1)} %get-tuple-element.471.info, f32[512,512]{1,0:T(8,128)S(1)} %copy-done.23, bf16[512,2048]{1,0:T(8,128)(2,1)S(1)} %copy-done.11, f32[512,128]{1,0:T(8,128)} %get-tuple-element.423.cos_ref, f32[512,128]{1,0:T(8,128)} %get-tuple-element.424.sin_ref, ...), custom_call_target="tpu_custom_call" | custom-call | flops 1073741824 | bytes 5242880 | tf_op jit(solution)/shard_map/cond/branch_2_fun/pallas_call | solution.py:570
  68.9 3.7 collective-permute-start.137
  74.7 3.9 %branch_2_fun.26 = bf16[4,80,2048]{2,1,0:T(8,128)(2,1)S(1)} custom-call(s32[26]{0:T(128)S(1)} %get-tuple-element.471.info, bf16[512,2048]{1,0:T(8,128)(2,1)} %get-tuple-element.419.w_ref, bf16[512,512]{1,0:T(8,128)(2,1)} %branch_2_fun.25.rest_0_, bf16[512,512]{1,0:T(8,128)(2,1)S(1)} %collective-permute-done.135.rest_1_, bf16[512,512]{1,0:T(8,128)(2,1)S(1)} %copy-done.49, ...), custom_call_target="tpu_custom_call" | custom-call | flops 1006632960 | bytes 4456448 | tf_op jit(solution)/shard_map/cond/branch_2_fun/pallas_call | solution.py:599
  80.5 4.7 %collective-permute-done.137 = bf16[128,2048]{1,0:T(8,128)(2,1)S(1)} collective-permute-done((bf16[128,2048]{1,0:T(8,128)(2,1)}, bf16[128,2048]{1,0:T(8,128)(2,1)S(1)}, u32[]{:S(2)}, u32[]{:S(2)}) %collective-permute-start.137) | collective-permute-done | bytes 524320 | tf_op jit(solution)/shard_map/cond/branch_2_fun/ppermute | solution.py:470
  85.9 5.1 %collective-permute-start.140 = (bf16[128,2048]{1,0:T(8,128)(2,1)S(1)}, bf16[128,2048]{1,0:T(8,128)(2,1)S(1)}, u32[]{:S(2)}, u32[]{:S(2)}) collective-permute-start(bf16[128,2048]{1,0:T(8,128)(2,1)S(1)} %get-tuple-element.455), channel_id=1, source_target_pairs={{0,1},{1,2},{4,5},{5,6},{8,9},{9,10},{12,13},{13,14},{16,17},{17,1... | collective-permute-start | bytes 1572872 | tf_op jit(solution)/shard_map/cond/branch_2_fun/ppermute | solution.py:488
  91.1 3.2 branch_2_fun.24
  95.3 5.1 %collective-permute-start.138 = (bf16[80,2048]{1,0:T(8,128)(2,1)S(1)}, bf16[80,2048]{1,0:T(8,128)(2,1)S(1)}, u32[]{:S(2)}, u32[]{:S(2)}) collective-permute-start(bf16[80,2048]{1,0:T(8,128)(2,1)S(1)} %get-tuple-element.458), channel_id=1, source_target_pairs={{0,1},{1,2},{4,5},{5,6},{8,9},{9,10},{12,13},{13,14},{16,17},{17,1... | collective-permute-start | bytes 983048 | tf_op jit(solution)/shard_map/cond/branch_2_fun/ppermute | solution.py:488
  100.5 2.8 collective-permute-done.140
  104.7 5.0 %collective-permute-start.145 = (bf16[128,2048]{1,0:T(8,128)(2,1)S(1)}, bf16[128,2048]{1,0:T(8,128)(2,1)S(1)}, u32[]{:S(2)}, u32[]{:S(2)}) collective-permute-start(bf16[128,2048]{1,0:T(8,128)(2,1)S(1)} %get-tuple-element.463), channel_id=1, source_target_pairs={{0,1},{1,2},{2,3},{4,5},{5,6},{6,7},{8,9},{9,10},{10,11},{12,13},{... | collective-permute-start | bytes 1572872 | tf_op jit(solution)/shard_map/cond/branch_2_fun/ppermute | solution.py:488
  111.2 7.5 %collective-permute-done.146.rest_2_ = bf16[128,2048]{1,0:T(8,128)(2,1)S(1)} collective-permute-done((bf16[128,2048]{1,0:T(8,128)(2,1)S(1)}, bf16[128,2048]{1,0:T(8,128)(2,1)S(1)}, u32[]{:S(2)}, u32[]{:S(2)}) %collective-permute-start.146) | collective-permute-done | bytes 524320 | tf_op jit(solution)/shard_map/cond/branch_2_fun/ppermute | solution.py:489
  118.7 2.2 collective-permute-done.145.rest_1_
  124.0 5.8 %collective-permute-start.149 = (bf16[128,2048]{1,0:T(8,128)(2,1)}, bf16[128,2048]{1,0:T(8,128)(2,1)}, u32[]{:S(2)}, u32[]{:S(2)}) collective-permute-start(bf16[128,2048]{1,0:T(8,128)(2,1)} %get-tuple-element.479.own), channel_id=1, source_target_pairs={{0,1},{1,2},{2,3},{4,5},{5,6},{6,7},{8,9},{9,10},{10,11},{12,13},{... | collective-permute-start | bytes 1572872 | tf_op jit(solution)/shard_map/cond/branch_2_fun/ppermute | solution.py:497
  131.1 4.6 %collective-permute-start.142 = (bf16[80,2048]{1,0:T(8,128)(2,1)S(1)}, bf16[80,2048]{1,0:T(8,128)(2,1)S(1)}, u32[]{:S(2)}, u32[]{:S(2)}) collective-permute-start(bf16[80,2048]{1,0:T(8,128)(2,1)S(1)} %get-tuple-element.466), channel_id=1, source_target_pairs={{0,1},{1,2},{2,3},{4,5},{5,6},{6,7},{8,9},{9,10},{10,11},{12,13},{... | collective-permute-start | bytes 983048 | tf_op jit(solution)/shard_map/cond/branch_2_fun/ppermute | solution.py:488
  135.7 9.6 %collective-permute-done.143.rest_2_ = bf16[80,2048]{1,0:T(8,128)(2,1)S(1)} collective-permute-done((bf16[80,2048]{1,0:T(8,128)(2,1)}, bf16[80,2048]{1,0:T(8,128)(2,1)S(1)}, u32[]{:S(2)}, u32[]{:S(2)}) %collective-permute-start.143) | collective-permute-done | bytes 327712 | tf_op jit(solution)/shard_map/cond/branch_2_fun/ppermute | solution.py:489
  150.8 8.9 %collective-permute-start.147 = (bf16[80,2048]{1,0:T(8,128)(2,1)S(1)}, bf16[80,2048]{1,0:T(8,128)(2,1)S(1)}, u32[]{:S(2)}, u32[]{:S(2)}) collective-permute-start(bf16[80,2048]{1,0:T(8,128)(2,1)S(1)} %get-tuple-element.478.own), channel_id=1, source_target_pairs={{0,1},{1,2},{2,3},{4,5},{5,6},{6,7},{8,9},{9,10},{10,11},{12,13},{... | collective-permute-start | bytes 983048 | tf_op jit(solution)/shard_map/cond/branch_2_fun/ppermute | solution.py:497
  159.8 9.5 %collective-permute-done.148.rest_3_ = bf16[80,2048]{1,0:T(8,128)(2,1)S(1)} collective-permute-done((bf16[80,2048]{1,0:T(8,128)(2,1)S(1)}, bf16[80,2048]{1,0:T(8,128)(2,1)S(1)}, u32[]{:S(2)}, u32[]{:S(2)}) %collective-permute-start.148) | collective-permute-done | bytes 327712 | tf_op jit(solution)/shard_map/cond/branch_2_fun/ppermute | solution.py:498
  172.6 8.9 %collective-permute-done.152.rest_4_ = bf16[80,2048]{1,0:T(8,128)(2,1)S(1)} collective-permute-done((bf16[80,2048]{1,0:T(8,128)(2,1)S(1)}, bf16[80,2048]{1,0:T(8,128)(2,1)S(1)}, u32[]{:S(2)}, u32[]{:S(2)}) %collective-permute-start.152) | collective-permute-done | bytes 327712 | tf_op jit(solution)/shard_map/cond/branch_2_fun/ppermute | solution.py:498
  182.9 9.9 %collective-permute-done.156.rest_2_.rest_5_ = bf16[128,2048]{1,0:T(8,128)(2,1)S(1)} collective-permute-done((bf16[128,2048]{1,0:T(8,128)(2,1)S(1)}, bf16[128,2048]{1,0:T(8,128)(2,1)S(1)}, u32[]{:S(2)}, u32[]{:S(2)}) %collective-permute-start.156) | collective-permute-done | bytes 524320 | tf_op jit(solution)/shard_map/cond/branch_2_fun/ppermute | solution.py:501
  192.8 4.6 %copy-done.2 = bf16[32,768,256]{2,1,0:T(8,128)(2,1)S(1)} copy-done((bf16[32,768,256]{2,1,0:T(8,128)(2,1)S(1)}, bf16[32,768,256]{2,1,0:T(8,128)(2,1)}, u32[]{:S(2)}) %copy-start.2) | copy-done | bytes 12582936 | tf_op jit(solution)/shard_map/cond
  197.4 10.7 %branch_2_fun.30 = bf16[4,128,2048]{2,1,0:T(8,128)(2,1)S(1)} custom-call(s32[26]{0:T(128)S(1)} %get-tuple-element.471.info, bf16[128,2048]{1,0:T(8,128)(2,1)} %get-tuple-element.479.own, bf16[128,2048]{1,0:T(8,128)(2,1)} %collective-permute-done.149.rest_0_, bf16[128,2048]{1,0:T(8,128)(2,1)S(1)} %collective-permute-done.153.rest_1_, ...), custom_call_target="tpu_custom_call" | custom-call | flops 6442450944 | bytes 12582912 | tf_op jit(solution)/shard_map/cond/branch_2_fun/pallas_call | solution.py:670
  209.9 7.4 %branch_2_fun.29 = bf16[4,80,2048]{2,1,0:T(8,128)(2,1)S(1)} custom-call(s32[26]{0:T(128)S(1)} %get-tuple-element.471.info, bf16[80,2048]{1,0:T(8,128)(2,1)S(1)} %get-tuple-element.478.own, bf16[80,2048]{1,0:T(8,128)(2,1)S(1)} %collective-permute-done.147.rest_0_, bf16[80,2048]{1,0:T(8,128)(2,1)S(1)} %collective-permute-done.151.rest_1_, ...), custom_call_target="tpu_custom_call" | custom-call | flops 4026531840 | bytes 12582912 | tf_op jit(solution)/shard_map/cond/branch_2_fun/pallas_call | solution.py:670
  219.8 5.0 %collective-permute-start.161 = (bf16[128,2048]{1,0:T(8,128)(2,1)S(1)}, bf16[128,2048]{1,0:T(8,128)(2,1)S(1)}, u32[]{:S(2)}, u32[]{:S(2)}) collective-permute-start(bf16[128,2048]{1,0:T(8,128)(2,1)S(1)} %get-tuple-element.490), channel_id=1, source_target_pairs={{0,1},{1,2},{4,5},{5,6},{8,9},{9,10},{12,13},{13,14},{16,17},{17,1... | collective-permute-start | bytes 1572872 | tf_op jit(solution)/shard_map/cond/branch_2_fun/ppermute | solution.py:488
  227.6 9.7 %collective-permute-start.159 = (bf16[80,2048]{1,0:T(8,128)(2,1)S(1)}, bf16[80,2048]{1,0:T(8,128)(2,1)S(1)}, u32[]{:S(2)}, u32[]{:S(2)}) collective-permute-start(bf16[80,2048]{1,0:T(8,128)(2,1)S(1)} %get-tuple-element.493), channel_id=1, source_target_pairs={{0,1},{1,2},{4,5},{5,6},{8,9},{9,10},{12,13},{13,14},{16,17},{17,1... | collective-permute-start | bytes 983048 | tf_op jit(solution)/shard_map/cond/branch_2_fun/ppermute | solution.py:488
  239.4 5.8 %collective-permute-start.165 = (bf16[128,2048]{1,0:T(8,128)(2,1)S(1)}, bf16[128,2048]{1,0:T(8,128)(2,1)S(1)}, u32[]{:S(2)}, u32[]{:S(2)}) collective-permute-start(bf16[128,2048]{1,0:T(8,128)(2,1)S(1)} %get-tuple-element.498), channel_id=1, source_target_pairs={{0,1},{1,2},{2,3},{4,5},{5,6},{6,7},{8,9},{9,10},{10,11},{12,13},{... | collective-permute-start | bytes 1572872 | tf_op jit(solution)/shard_map/cond/branch_2_fun/ppermute | solution.py:488
  245.5 4.7 %collective-permute-done.166.rest_2_ = bf16[128,2048]{1,0:T(8,128)(2,1)S(1)} collective-permute-done((bf16[128,2048]{1,0:T(8,128)(2,1)S(1)}, bf16[128,2048]{1,0:T(8,128)(2,1)S(1)}, u32[]{:S(2)}, u32[]{:S(2)}) %collective-permute-start.166) | collective-permute-done | bytes 524320 | tf_op jit(solution)/shard_map/cond/branch_2_fun/ppermute | solution.py:489
  250.2 3.0 collective-permute-done.165.rest_1_
  255.6 8.3 %collective-permute-start.170 = (bf16[128,2048]{1,0:T(8,128)(2,1)S(1)}, bf16[128,2048]{1,0:T(8,128)(2,1)S(1)}, u32[]{:S(2)}, u32[]{:S(2)}) collective-permute-start(bf16[128,2048]{1,0:T(8,128)(2,1)S(1)} %get-tuple-element.512.own), channel_id=1, source_target_pairs={{0,1},{1,2},{2,3},{4,5},{5,6},{6,7},{8,9},{9,10},{10,11},{12,13},{... | collective-permute-start | bytes 1572872 | tf_op jit(solution)/shard_map/cond/branch_2_fun/ppermute | solution.py:497
  265.2 5.4 %collective-permute-start.163 = (bf16[80,2048]{1,0:T(8,128)(2,1)S(1)}, bf16[80,2048]{1,0:T(8,128)(2,1)S(1)}, u32[]{:S(2)}, u32[]{:S(2)}) collective-permute-start(bf16[80,2048]{1,0:T(8,128)(2,1)S(1)} %get-tuple-element.501), channel_id=1, source_target_pairs={{0,1},{1,2},{2,3},{4,5},{5,6},{6,7},{8,9},{9,10},{10,11},{12,13},{... | collective-permute-start | bytes 983048 | tf_op jit(solution)/shard_map/cond/branch_2_fun/ppermute | solution.py:488
  270.6 5.5 %collective-permute-done.164.rest_2_ = bf16[80,2048]{1,0:T(8,128)(2,1)S(1)} collective-permute-done((bf16[80,2048]{1,0:T(8,128)(2,1)S(1)}, bf16[80,2048]{1,0:T(8,128)(2,1)S(1)}, u32[]{:S(2)}, u32[]{:S(2)}) %collective-permute-start.164) | collective-permute-done | bytes 327712 | tf_op jit(solution)/shard_map/cond/branch_2_fun/ppermute | solution.py:489
  282.0 9.2 %collective-permute-start.167 = (bf16[80,2048]{1,0:T(8,128)(2,1)S(1)}, bf16[80,2048]{1,0:T(8,128)(2,1)S(1)}, u32[]{:S(2)}, u32[]{:S(2)}) collective-permute-start(bf16[80,2048]{1,0:T(8,128)(2,1)S(1)} %get-tuple-element.509.own), channel_id=1, source_target_pairs={{0,1},{1,2},{2,3},{4,5},{5,6},{6,7},{8,9},{9,10},{10,11},{12,13},{... | collective-permute-start | bytes 983048 | tf_op jit(solution)/shard_map/cond/branch_2_fun/ppermute | solution.py:497
  292.7 2.8 collective-permute-done.169
  306.7 10.9 %collective-permute-done.173.rest_4_ = bf16[80,2048]{1,0:T(8,128)(2,1)S(1)} collective-permute-done((bf16[80,2048]{1,0:T(8,128)(2,1)S(1)}, bf16[80,2048]{1,0:T(8,128)(2,1)S(1)}, u32[]{:S(2)}, u32[]{:S(2)}) %collective-permute-start.173) | collective-permute-done | bytes 327712 | tf_op jit(solution)/shard_map/cond/branch_2_fun/ppermute | solution.py:498
  319.0 4.0 %collective-permute-done.180 = bf16[16,2048]{1,0:T(8,128)(2,1)S(1)} collective-permute-done((bf16[16,2048]{1,0:T(8,128)(2,1)S(1)}, bf16[16,2048]{1,0:T(8,128)(2,1)S(1)}, u32[]{:S(2)}, u32[]{:S(2)}) %collective-permute-start.180) | collective-permute-done | bytes 65568 | tf_op jit(solution)/shard_map/cond/branch_2_fun/ppermute | solution.py:716
  326.3 3.7 %collective-permute-done.183 = bf16[16,2048]{1,0:T(8,128)(2,1)S(1)} collective-permute-done((bf16[16,2048]{1,0:T(8,128)(2,1)S(1)}, bf16[16,2048]{1,0:T(8,128)(2,1)S(1)}, u32[]{:S(2)}, u32[]{:S(2)}) %collective-permute-start.183) | collective-permute-done | bytes 65568 | tf_op jit(solution)/shard_map/cond/branch_2_fun/ppermute | solution.py:716
  330.1 2.7 branch_2_fun.37
  335.4 2.2 collective-permute-done.184
  339.1 2.3 collective-permute-done.185
  341.5 3.6 collective-permute-done.186
  345.6 4.1 %collective-permute-done.187 = f32[16,128]{1,0:T(8,128)S(1)} collective-permute-done((f32[16,128]{1,0:T(8,128)S(1)}, f32[16,128]{1,0:T(8,128)S(1)}, u32[]{:S(2)}, u32[]{:S(2)}) %collective-permute-start.187) | collective-permute-done | bytes 8224 | tf_op jit(solution)/shard_map/cond/branch_2_fun/ppermute | solution.py:775
  (198 shorter events, 86.0 us)
Async XLA Ops:
  15.4 120.3 %all-gather.13.cloned.1.call-start = ((), (), s32[]{:S(2)}) async-start(), calls=%async_computation.2 | async-start | bytes 14155776 | tf_op jit(solution)/shard_map/cond/branch_2_fun/all_gather | solution.py:622
  15.5 15.4 %collective-permute-start.126 = (bf16[2,16,2560]{2,1,0:T(8,128)(2,1)S(1)}, bf16[2,16,2560]{2,1,0:T(8,128)(2,1)S(1)}, u32[]{:S(2)}, u32[]{:S(2)}) collective-permute-start(bf16[2,16,2560]{2,1,0:T(8,128)(2,1)S(1)} %get-tuple-element.432), channel_id=1, source_target_pairs={{0,4},{4,0},{8,12},{12,8},{16,20},{20,16},{24,28},{28,24},{1,5},{5... | collective-permute-start | bytes 491528 | tf_op jit(solution)/shard_map/cond/branch_2_fun/ppermute | solution.py:529
  16.0 17.5 %collective-permute-start.127 = (bf16[2,16,2560]{2,1,0:T(8,128)(2,1)S(1)}, bf16[2,16,2560]{2,1,0:T(8,128)(2,1)S(1)}, u32[]{:S(2)}, u32[]{:S(2)}) collective-permute-start(bf16[2,16,2560]{2,1,0:T(8,128)(2,1)S(1)} %get-tuple-element.433), channel_id=1, source_target_pairs={{0,8},{4,12},{8,0},{12,4},{16,24},{20,28},{24,16},{28,20},{1,9},{5... | collective-permute-start | bytes 491528 | tf_op jit(solution)/shard_map/cond/branch_2_fun/ppermute | solution.py:529
  18.6 19.5 %collective-permute-start.128 = (bf16[2,16,2560]{2,1,0:T(8,128)(2,1)S(1)}, bf16[2,16,2560]{2,1,0:T(8,128)(2,1)S(1)}, u32[]{:S(2)}, u32[]{:S(2)}) collective-permute-start(bf16[2,16,2560]{2,1,0:T(8,128)(2,1)S(1)} %get-tuple-element.434), channel_id=1, source_target_pairs={{0,12},{4,8},{8,4},{12,0},{16,28},{20,24},{24,20},{28,16},{1,13},{... | collective-permute-start | bytes 491528 | tf_op jit(solution)/shard_map/cond/branch_2_fun/ppermute | solution.py:529
  18.6 19.4 %collective-permute-start.129 = (bf16[2,16,2560]{2,1,0:T(8,128)(2,1)S(1)}, bf16[2,16,2560]{2,1,0:T(8,128)(2,1)S(1)}, u32[]{:S(2)}, u32[]{:S(2)}) collective-permute-start(bf16[2,16,2560]{2,1,0:T(8,128)(2,1)S(1)} %get-tuple-element.435), channel_id=1, source_target_pairs={{0,16},{4,20},{8,24},{12,28},{16,0},{20,4},{24,8},{28,12},{1,17},{... | collective-permute-start | bytes 491528 | tf_op jit(solution)/shard_map/cond/branch_2_fun/ppermute | solution.py:529
  20.4 17.6 %collective-permute-start.130 = (bf16[2,16,2560]{2,1,0:T(8,128)(2,1)S(1)}, bf16[2,16,2560]{2,1,0:T(8,128)(2,1)S(1)}, u32[]{:S(2)}, u32[]{:S(2)}) collective-permute-start(bf16[2,16,2560]{2,1,0:T(8,128)(2,1)S(1)} %get-tuple-element.436), channel_id=1, source_target_pairs={{0,20},{4,16},{8,28},{12,24},{16,4},{20,0},{24,12},{28,8},{1,21},{... | collective-permute-start | bytes 491528 | tf_op jit(solution)/shard_map/cond/branch_2_fun/ppermute | solution.py:529
  68.9 16.3 %collective-permute-start.137 = (bf16[128,2048]{1,0:T(8,128)(2,1)}, bf16[128,2048]{1,0:T(8,128)(2,1)S(1)}, u32[]{:S(2)}, u32[]{:S(2)}) collective-permute-start(bf16[128,2048]{1,0:T(8,128)(2,1)} %get-tuple-element.751), channel_id=1, source_target_pairs={{0,1},{3,2},{4,5},{7,6},{8,9},{11,10},{12,13},{15,14},{16,17},{19,... | collective-permute-start | bytes 1572872 | tf_op jit(solution)/shard_map/cond/branch_2_fun/ppermute | solution.py:470
  78.7 15.7 %collective-permute-start.136 = (bf16[80,2048]{1,0:T(8,128)(2,1)S(1)}, bf16[80,2048]{1,0:T(8,128)(2,1)S(1)}, u32[]{:S(2)}, u32[]{:S(2)}) collective-permute-start(bf16[80,2048]{1,0:T(8,128)(2,1)S(1)} %get-tuple-element.452), channel_id=1, source_target_pairs={{0,1},{3,2},{4,5},{7,6},{8,9},{11,10},{12,13},{15,14},{16,17},{19,... | collective-permute-start | bytes 983048 | tf_op jit(solution)/shard_map/cond/branch_2_fun/ppermute | solution.py:470
  85.2 15.3 %collective-permute-start.141 = (bf16[128,2048]{1,0:T(8,128)(2,1)S(1)}, bf16[128,2048]{1,0:T(8,128)(2,1)S(1)}, u32[]{:S(2)}, u32[]{:S(2)}) collective-permute-start(bf16[128,2048]{1,0:T(8,128)(2,1)S(1)} %get-tuple-element.460), channel_id=1, source_target_pairs={{3,2},{2,1},{7,6},{6,5},{11,10},{10,9},{15,14},{14,13},{19,18},{18... | collective-permute-start | bytes 1572872 | tf_op jit(solution)/shard_map/cond/branch_2_fun/ppermute | solution.py:489
  85.9 17.4 %collective-permute-start.140 = (bf16[128,2048]{1,0:T(8,128)(2,1)S(1)}, bf16[128,2048]{1,0:T(8,128)(2,1)S(1)}, u32[]{:S(2)}, u32[]{:S(2)}) collective-permute-start(bf16[128,2048]{1,0:T(8,128)(2,1)S(1)} %get-tuple-element.455), channel_id=1, source_target_pairs={{0,1},{1,2},{4,5},{5,6},{8,9},{9,10},{12,13},{13,14},{16,17},{17,1... | collective-permute-start | bytes 1572872 | tf_op jit(solution)/shard_map/cond/branch_2_fun/ppermute | solution.py:488
  94.3 16.8 %collective-permute-start.144 = (bf16[128,2048]{1,0:T(8,128)(2,1)S(1)}, bf16[128,2048]{1,0:T(8,128)(2,1)S(1)}, u32[]{:S(2)}, u32[]{:S(2)}) collective-permute-start(bf16[128,2048]{1,0:T(8,128)(2,1)S(1)} %get-tuple-element.473), channel_id=1, source_target_pairs={{0,4},{4,0},{8,12},{12,8},{16,20},{20,16},{24,28},{28,24},{1,5},{5... | collective-permute-start | bytes 1572872 | tf_op jit(solution)/shard_map/cond/branch_2_fun/ppermute | solution.py:635
  94.5 15.3 %collective-permute-start.139 = (bf16[80,2048]{1,0:T(8,128)(2,1)S(1)}, bf16[80,2048]{1,0:T(8,128)(2,1)S(1)}, u32[]{:S(2)}, u32[]{:S(2)}) collective-permute-start(bf16[80,2048]{1,0:T(8,128)(2,1)S(1)} %get-tuple-element.459), channel_id=1, source_target_pairs={{3,2},{2,1},{7,6},{6,5},{11,10},{10,9},{15,14},{14,13},{19,18},{18... | collective-permute-start | bytes 983048 | tf_op jit(solution)/shard_map/cond/branch_2_fun/ppermute | solution.py:489
  95.3 15.0 %collective-permute-start.138 = (bf16[80,2048]{1,0:T(8,128)(2,1)S(1)}, bf16[80,2048]{1,0:T(8,128)(2,1)S(1)}, u32[]{:S(2)}, u32[]{:S(2)}) collective-permute-start(bf16[80,2048]{1,0:T(8,128)(2,1)S(1)} %get-tuple-element.458), channel_id=1, source_target_pairs={{0,1},{1,2},{4,5},{5,6},{8,9},{9,10},{12,13},{13,14},{16,17},{17,1... | collective-permute-start | bytes 983048 | tf_op jit(solution)/shard_map/cond/branch_2_fun/ppermute | solution.py:488
  103.4 15.2 %collective-permute-start.146 = (bf16[128,2048]{1,0:T(8,128)(2,1)S(1)}, bf16[128,2048]{1,0:T(8,128)(2,1)S(1)}, u32[]{:S(2)}, u32[]{:S(2)}) collective-permute-start(bf16[128,2048]{1,0:T(8,128)(2,1)S(1)} %get-tuple-element.474), channel_id=1, source_target_pairs={{3,2},{2,1},{1,0},{7,6},{6,5},{5,4},{11,10},{10,9},{9,8},{15,14},{... | collective-permute-start | bytes 1572872 | tf_op jit(solution)/shard_map/cond/branch_2_fun/ppermute | solution.py:489
  104.7 16.1 %collective-permute-start.145 = (bf16[128,2048]{1,0:T(8,128)(2,1)S(1)}, bf16[128,2048]{1,0:T(8,128)(2,1)S(1)}, u32[]{:S(2)}, u32[]{:S(2)}) collective-permute-start(bf16[128,2048]{1,0:T(8,128)(2,1)S(1)} %get-tuple-element.463), channel_id=1, source_target_pairs={{0,1},{1,2},{2,3},{4,5},{5,6},{6,7},{8,9},{9,10},{10,11},{12,13},{... | collective-permute-start | bytes 1572872 | tf_op jit(solution)/shard_map/cond/branch_2_fun/ppermute | solution.py:488
  122.7 24.8 %collective-permute-start.150 = (bf16[128,2048]{1,0:T(8,128)(2,1)}, bf16[128,2048]{1,0:T(8,128)(2,1)}, u32[]{:S(2)}, u32[]{:S(2)}) collective-permute-start(bf16[128,2048]{1,0:T(8,128)(2,1)} %get-tuple-element.479.own), channel_id=1, source_target_pairs={{1,0},{2,1},{3,2},{5,4},{6,5},{7,6},{9,8},{10,9},{11,10},{13,12},{... | collective-permute-start | bytes 1572872 | tf_op jit(solution)/shard_map/cond/branch_2_fun/ppermute | solution.py:498
  124.0 23.5 %collective-permute-start.149 = (bf16[128,2048]{1,0:T(8,128)(2,1)}, bf16[128,2048]{1,0:T(8,128)(2,1)}, u32[]{:S(2)}, u32[]{:S(2)}) collective-permute-start(bf16[128,2048]{1,0:T(8,128)(2,1)} %get-tuple-element.479.own), channel_id=1, source_target_pairs={{0,1},{1,2},{2,3},{4,5},{5,6},{6,7},{8,9},{9,10},{10,11},{12,13},{... | collective-permute-start | bytes 1572872 | tf_op jit(solution)/shard_map/cond/branch_2_fun/ppermute | solution.py:497
  129.8 15.5 %collective-permute-start.143 = (bf16[80,2048]{1,0:T(8,128)(2,1)}, bf16[80,2048]{1,0:T(8,128)(2,1)S(1)}, u32[]{:S(2)}, u32[]{:S(2)}) collective-permute-start(bf16[80,2048]{1,0:T(8,128)(2,1)} %get-tuple-element.467), channel_id=1, source_target_pairs={{3,2},{2,1},{1,0},{7,6},{6,5},{5,4},{11,10},{10,9},{9,8},{15,14},{... | collective-permute-start | bytes 983048 | tf_op jit(solution)/shard_map/cond/branch_2_fun/ppermute | solution.py:489
  131.1 15.4 %collective-permute-start.142 = (bf16[80,2048]{1,0:T(8,128)(2,1)S(1)}, bf16[80,2048]{1,0:T(8,128)(2,1)S(1)}, u32[]{:S(2)}, u32[]{:S(2)}) collective-permute-start(bf16[80,2048]{1,0:T(8,128)(2,1)S(1)} %get-tuple-element.466), channel_id=1, source_target_pairs={{0,1},{1,2},{2,3},{4,5},{5,6},{6,7},{8,9},{9,10},{10,11},{12,13},{... | collective-permute-start | bytes 983048 | tf_op jit(solution)/shard_map/cond/branch_2_fun/ppermute | solution.py:488
  147.5 23.7 %collective-permute-start.154 = (bf16[128,2048]{1,0:T(8,128)(2,1)}, bf16[128,2048]{1,0:T(8,128)(2,1)S(1)}, u32[]{:S(2)}, u32[]{:S(2)}) collective-permute-start(bf16[128,2048]{1,0:T(8,128)(2,1)} %collective-permute-done.150.rest_3_), channel_id=1, source_target_pairs={{1,0},{2,1},{5,4},{6,5},{9,8},{10,9},{13,12},{14,13},{17,16},{18,1... | collective-permute-start | bytes 1572872 | tf_op jit(solution)/shard_map/cond/branch_2_fun/ppermute | solution.py:498
  148.8 22.4 %collective-permute-start.153 = (bf16[128,2048]{1,0:T(8,128)(2,1)}, bf16[128,2048]{1,0:T(8,128)(2,1)S(1)}, u32[]{:S(2)}, u32[]{:S(2)}) collective-permute-start(bf16[128,2048]{1,0:T(8,128)(2,1)} %collective-permute-done.149.rest_0_), channel_id=1, source_target_pairs={{1,2},{2,3},{5,6},{6,7},{9,10},{10,11},{13,14},{14,15},{17,18},{18... | collective-permute-start | bytes 1572872 | tf_op jit(solution)/shard_map/cond/branch_2_fun/ppermute | solution.py:497
  149.5 19.7 %collective-permute-start.148 = (bf16[80,2048]{1,0:T(8,128)(2,1)S(1)}, bf16[80,2048]{1,0:T(8,128)(2,1)S(1)}, u32[]{:S(2)}, u32[]{:S(2)}) collective-permute-start(bf16[80,2048]{1,0:T(8,128)(2,1)S(1)} %get-tuple-element.478.own), channel_id=1, source_target_pairs={{1,0},{2,1},{3,2},{5,4},{6,5},{7,6},{9,8},{10,9},{11,10},{13,12},{... | collective-permute-start | bytes 983048 | tf_op jit(solution)/shard_map/cond/branch_2_fun/ppermute | solution.py:498
  150.8 18.4 %collective-permute-start.147 = (bf16[80,2048]{1,0:T(8,128)(2,1)S(1)}, bf16[80,2048]{1,0:T(8,128)(2,1)S(1)}, u32[]{:S(2)}, u32[]{:S(2)}) collective-permute-start(bf16[80,2048]{1,0:T(8,128)(2,1)S(1)} %get-tuple-element.478.own), channel_id=1, source_target_pairs={{0,1},{1,2},{2,3},{4,5},{5,6},{6,7},{8,9},{9,10},{10,11},{12,13},{... | collective-permute-start | bytes 983048 | tf_op jit(solution)/shard_map/cond/branch_2_fun/ppermute | solution.py:497
  169.2 12.3 %collective-permute-start.152 = (bf16[80,2048]{1,0:T(8,128)(2,1)S(1)}, bf16[80,2048]{1,0:T(8,128)(2,1)S(1)}, u32[]{:S(2)}, u32[]{:S(2)}) collective-permute-start(bf16[80,2048]{1,0:T(8,128)(2,1)S(1)} %collective-permute-done.148.rest_3_), channel_id=1, source_target_pairs={{1,0},{2,1},{5,4},{6,5},{9,8},{10,9},{13,12},{14,13},{17,16},{18,1... | collective-permute-start | bytes 983048 | tf_op jit(solution)/shard_map/cond/branch_2_fun/ppermute | solution.py:498
  170.5 11.0 %collective-permute-start.151 = (bf16[80,2048]{1,0:T(8,128)(2,1)S(1)}, bf16[80,2048]{1,0:T(8,128)(2,1)S(1)}, u32[]{:S(2)}, u32[]{:S(2)}) collective-permute-start(bf16[80,2048]{1,0:T(8,128)(2,1)S(1)} %collective-permute-done.147.rest_0_), channel_id=1, source_target_pairs={{1,2},{2,3},{5,6},{6,7},{9,10},{10,11},{13,14},{14,15},{17,18},{18... | collective-permute-start | bytes 983048 | tf_op jit(solution)/shard_map/cond/branch_2_fun/ppermute | solution.py:497
  171.3 21.5 %collective-permute-start.156 = (bf16[128,2048]{1,0:T(8,128)(2,1)S(1)}, bf16[128,2048]{1,0:T(8,128)(2,1)S(1)}, u32[]{:S(2)}, u32[]{:S(2)}) collective-permute-start(bf16[128,2048]{1,0:T(8,128)(2,1)S(1)} %broadcast_select_fusion.9), channel_id=1, source_target_pairs={{2,3},{1,0},{6,7},{5,4},{10,11},{9,8},{14,15},{13,12},{18,19},{17,... | collective-permute-start | bytes 1572872 | tf_op jit(solution)/shard_map/cond/branch_2_fun/ppermute | solution.py:501
  181.6 28.3 %collective-permute-start.155 = (bf16[80,2048]{1,0:T(8,128)(2,1)S(1)}, bf16[80,2048]{1,0:T(8,128)(2,1)S(1)}, u32[]{:S(2)}, u32[]{:S(2)}) collective-permute-start(bf16[80,2048]{1,0:T(8,128)(2,1)S(1)} %broadcast_select_fusion.11), channel_id=1, source_target_pairs={{2,3},{1,0},{6,7},{5,4},{10,11},{9,8},{14,15},{13,12},{18,19},{17,... | collective-permute-start | bytes 983048 | tf_op jit(solution)/shard_map/cond/branch_2_fun/ppermute | solution.py:501
  208.2 10.8 %collective-permute-start.158 = (bf16[128,2048]{1,0:T(8,128)(2,1)S(1)}, bf16[128,2048]{1,0:T(8,128)(2,1)S(1)}, u32[]{:S(2)}, u32[]{:S(2)}) collective-permute-start(bf16[128,2048]{1,0:T(8,128)(2,1)S(1)} %get-tuple-element.486), channel_id=1, source_target_pairs={{0,1},{3,2},{4,5},{7,6},{8,9},{11,10},{12,13},{15,14},{16,17},{19,... | collective-permute-start | bytes 1572872 | tf_op jit(solution)/shard_map/cond/branch_2_fun/ppermute | solution.py:470
  219.1 18.2 %collective-permute-start.162 = (bf16[128,2048]{1,0:T(8,128)(2,1)S(1)}, bf16[128,2048]{1,0:T(8,128)(2,1)S(1)}, u32[]{:S(2)}, u32[]{:S(2)}) collective-permute-start(bf16[128,2048]{1,0:T(8,128)(2,1)S(1)} %get-tuple-element.495), channel_id=1, source_target_pairs={{3,2},{2,1},{7,6},{6,5},{11,10},{10,9},{15,14},{14,13},{19,18},{18... | collective-permute-start | bytes 1572872 | tf_op jit(solution)/shard_map/cond/branch_2_fun/ppermute | solution.py:489
  219.8 18.2 %collective-permute-start.161 = (bf16[128,2048]{1,0:T(8,128)(2,1)S(1)}, bf16[128,2048]{1,0:T(8,128)(2,1)S(1)}, u32[]{:S(2)}, u32[]{:S(2)}) collective-permute-start(bf16[128,2048]{1,0:T(8,128)(2,1)S(1)} %get-tuple-element.490), channel_id=1, source_target_pairs={{0,1},{1,2},{4,5},{5,6},{8,9},{9,10},{12,13},{13,14},{16,17},{17,1... | collective-permute-start | bytes 1572872 | tf_op jit(solution)/shard_map/cond/branch_2_fun/ppermute | solution.py:488
  226.9 18.4 %collective-permute-start.160 = (bf16[80,2048]{1,0:T(8,128)(2,1)S(1)}, bf16[80,2048]{1,0:T(8,128)(2,1)S(1)}, u32[]{:S(2)}, u32[]{:S(2)}) collective-permute-start(bf16[80,2048]{1,0:T(8,128)(2,1)S(1)} %get-tuple-element.494), channel_id=1, source_target_pairs={{3,2},{2,1},{7,6},{6,5},{11,10},{10,9},{15,14},{14,13},{19,18},{18... | collective-permute-start | bytes 983048 | tf_op jit(solution)/shard_map/cond/branch_2_fun/ppermute | solution.py:489
  227.6 17.9 %collective-permute-start.159 = (bf16[80,2048]{1,0:T(8,128)(2,1)S(1)}, bf16[80,2048]{1,0:T(8,128)(2,1)S(1)}, u32[]{:S(2)}, u32[]{:S(2)}) collective-permute-start(bf16[80,2048]{1,0:T(8,128)(2,1)S(1)} %get-tuple-element.493), channel_id=1, source_target_pairs={{0,1},{1,2},{4,5},{5,6},{8,9},{9,10},{12,13},{13,14},{16,17},{17,1... | collective-permute-start | bytes 983048 | tf_op jit(solution)/shard_map/cond/branch_2_fun/ppermute | solution.py:488
  238.1 12.0 %collective-permute-start.166 = (bf16[128,2048]{1,0:T(8,128)(2,1)S(1)}, bf16[128,2048]{1,0:T(8,128)(2,1)S(1)}, u32[]{:S(2)}, u32[]{:S(2)}) collective-permute-start(bf16[128,2048]{1,0:T(8,128)(2,1)S(1)} %get-tuple-element.505), channel_id=1, source_target_pairs={{3,2},{2,1},{1,0},{7,6},{6,5},{5,4},{11,10},{10,9},{9,8},{15,14},{... | collective-permute-start | bytes 1572872 | tf_op jit(solution)/shard_map/cond/branch_2_fun/ppermute | solution.py:489
  239.4 13.7 %collective-permute-start.165 = (bf16[128,2048]{1,0:T(8,128)(2,1)S(1)}, bf16[128,2048]{1,0:T(8,128)(2,1)S(1)}, u32[]{:S(2)}, u32[]{:S(2)}) collective-permute-start(bf16[128,2048]{1,0:T(8,128)(2,1)S(1)} %get-tuple-element.498), channel_id=1, source_target_pairs={{0,1},{1,2},{2,3},{4,5},{5,6},{6,7},{8,9},{9,10},{10,11},{12,13},{... | collective-permute-start | bytes 1572872 | tf_op jit(solution)/shard_map/cond/branch_2_fun/ppermute | solution.py:488
  254.3 24.4 %collective-permute-start.171 = (bf16[128,2048]{1,0:T(8,128)(2,1)S(1)}, bf16[128,2048]{1,0:T(8,128)(2,1)S(1)}, u32[]{:S(2)}, u32[]{:S(2)}) collective-permute-start(bf16[128,2048]{1,0:T(8,128)(2,1)S(1)} %get-tuple-element.512.own), channel_id=1, source_target_pairs={{1,0},{2,1},{3,2},{5,4},{6,5},{7,6},{9,8},{10,9},{11,10},{13,12},{... | collective-permute-start | bytes 1572872 | tf_op jit(solution)/shard_map/cond/branch_2_fun/ppermute | solution.py:498
  255.6 23.1 %collective-permute-start.170 = (bf16[128,2048]{1,0:T(8,128)(2,1)S(1)}, bf16[128,2048]{1,0:T(8,128)(2,1)S(1)}, u32[]{:S(2)}, u32[]{:S(2)}) collective-permute-start(bf16[128,2048]{1,0:T(8,128)(2,1)S(1)} %get-tuple-element.512.own), channel_id=1, source_target_pairs={{0,1},{1,2},{2,3},{4,5},{5,6},{6,7},{8,9},{9,10},{10,11},{12,13},{... | collective-permute-start | bytes 1572872 | tf_op jit(solution)/shard_map/cond/branch_2_fun/ppermute | solution.py:497
  263.9 12.2 %collective-permute-start.164 = (bf16[80,2048]{1,0:T(8,128)(2,1)S(1)}, bf16[80,2048]{1,0:T(8,128)(2,1)S(1)}, u32[]{:S(2)}, u32[]{:S(2)}) collective-permute-start(bf16[80,2048]{1,0:T(8,128)(2,1)S(1)} %get-tuple-element.502), channel_id=1, source_target_pairs={{3,2},{2,1},{1,0},{7,6},{6,5},{5,4},{11,10},{10,9},{9,8},{15,14},{... | collective-permute-start | bytes 983048 | tf_op jit(solution)/shard_map/cond/branch_2_fun/ppermute | solution.py:489
  265.2 12.4 %collective-permute-start.163 = (bf16[80,2048]{1,0:T(8,128)(2,1)S(1)}, bf16[80,2048]{1,0:T(8,128)(2,1)S(1)}, u32[]{:S(2)}, u32[]{:S(2)}) collective-permute-start(bf16[80,2048]{1,0:T(8,128)(2,1)S(1)} %get-tuple-element.501), channel_id=1, source_target_pairs={{0,1},{1,2},{2,3},{4,5},{5,6},{6,7},{8,9},{9,10},{10,11},{12,13},{... | collective-permute-start | bytes 983048 | tf_op jit(solution)/shard_map/cond/branch_2_fun/ppermute | solution.py:488
  278.7 26.3 %collective-permute-start.175 = (bf16[128,2048]{1,0:T(8,128)(2,1)S(1)}, bf16[128,2048]{1,0:T(8,128)(2,1)S(1)}, u32[]{:S(2)}, u32[]{:S(2)}) collective-permute-start(bf16[128,2048]{1,0:T(8,128)(2,1)S(1)} %collective-permute-done.171.rest_3_), channel_id=1, source_target_pairs={{1,0},{2,1},{5,4},{6,5},{9,8},{10,9},{13,12},{14,13},{17,16},{18,1... | collective-permute-start | bytes 1572872 | tf_op jit(solution)/shard_map/cond/branch_2_fun/ppermute | solution.py:498
  280.0 25.1 %collective-permute-start.174 = (bf16[128,2048]{1,0:T(8,128)(2,1)S(1)}, bf16[128,2048]{1,0:T(8,128)(2,1)S(1)}, u32[]{:S(2)}, u32[]{:S(2)}) collective-permute-start(bf16[128,2048]{1,0:T(8,128)(2,1)S(1)} %collective-permute-done.170.rest_0_), channel_id=1, source_target_pairs={{1,2},{2,3},{5,6},{6,7},{9,10},{10,11},{13,14},{14,15},{17,18},{18... | collective-permute-start | bytes 1572872 | tf_op jit(solution)/shard_map/cond/branch_2_fun/ppermute | solution.py:497
  280.7 17.3 %collective-permute-start.168 = (bf16[80,2048]{1,0:T(8,128)(2,1)S(1)}, bf16[80,2048]{1,0:T(8,128)(2,1)S(1)}, u32[]{:S(2)}, u32[]{:S(2)}) collective-permute-start(bf16[80,2048]{1,0:T(8,128)(2,1)S(1)} %get-tuple-element.509.own), channel_id=1, source_target_pairs={{1,0},{2,1},{3,2},{5,4},{6,5},{7,6},{9,8},{10,9},{11,10},{13,12},{... | collective-permute-start | bytes 983048 | tf_op jit(solution)/shard_map/cond/branch_2_fun/ppermute | solution.py:498
  282.0 16.0 %collective-permute-start.167 = (bf16[80,2048]{1,0:T(8,128)(2,1)S(1)}, bf16[80,2048]{1,0:T(8,128)(2,1)S(1)}, u32[]{:S(2)}, u32[]{:S(2)}) collective-permute-start(bf16[80,2048]{1,0:T(8,128)(2,1)S(1)} %get-tuple-element.509.own), channel_id=1, source_target_pairs={{0,1},{1,2},{2,3},{4,5},{5,6},{6,7},{8,9},{9,10},{10,11},{12,13},{... | collective-permute-start | bytes 983048 | tf_op jit(solution)/shard_map/cond/branch_2_fun/ppermute | solution.py:497
  302.0 15.6 %collective-permute-start.172 = (bf16[80,2048]{1,0:T(8,128)(2,1)S(1)}, bf16[80,2048]{1,0:T(8,128)(2,1)S(1)}, u32[]{:S(2)}, u32[]{:S(2)}) collective-permute-start(bf16[80,2048]{1,0:T(8,128)(2,1)S(1)} %collective-permute-done.167.rest_0_), channel_id=1, source_target_pairs={{1,2},{2,3},{5,6},{6,7},{9,10},{10,11},{13,14},{14,15},{17,18},{18... | collective-permute-start | bytes 983048 | tf_op jit(solution)/shard_map/cond/branch_2_fun/ppermute | solution.py:497
  302.7 14.9 %collective-permute-start.173 = (bf16[80,2048]{1,0:T(8,128)(2,1)S(1)}, bf16[80,2048]{1,0:T(8,128)(2,1)S(1)}, u32[]{:S(2)}, u32[]{:S(2)}) collective-permute-start(bf16[80,2048]{1,0:T(8,128)(2,1)S(1)} %collective-permute-done.168.rest_3_), channel_id=1, source_target_pairs={{1,0},{2,1},{5,4},{6,5},{9,8},{10,9},{13,12},{14,13},{17,16},{18,1... | collective-permute-start | bytes 983048 | tf_op jit(solution)/shard_map/cond/branch_2_fun/ppermute | solution.py:498
  305.1 19.7 %collective-permute-start.178 = (bf16[128,2048]{1,0:T(8,128)(2,1)S(1)}, bf16[128,2048]{1,0:T(8,128)(2,1)S(1)}, u32[]{:S(2)}, u32[]{:S(2)}) collective-permute-start(bf16[128,2048]{1,0:T(8,128)(2,1)S(1)} %broadcast_select_fusion.8), channel_id=1, source_target_pairs={{2,3},{1,0},{6,7},{5,4},{10,11},{9,8},{14,15},{13,12},{18,19},{17,... | collective-permute-start | bytes 1572872 | tf_op jit(solution)/shard_map/cond/branch_2_fun/ppermute | solution.py:501
  317.7 15.1 %collective-permute-start.177 = (bf16[80,2048]{1,0:T(8,128)(2,1)S(1)}, bf16[80,2048]{1,0:T(8,128)(2,1)S(1)}, u32[]{:S(2)}, u32[]{:S(2)}) collective-permute-start(bf16[80,2048]{1,0:T(8,128)(2,1)S(1)} %broadcast_select_fusion.10), channel_id=1, source_target_pairs={{2,3},{1,0},{6,7},{5,4},{10,11},{9,8},{14,15},{13,12},{18,19},{17,... | collective-permute-start | bytes 983048 | tf_op jit(solution)/shard_map/cond/branch_2_fun/ppermute | solution.py:501
  325.7 26.5 %collective-permute-start.182 = (bf16[512,2048]{1,0:T(8,128)(2,1)S(1)}, bf16[512,2048]{1,0:T(8,128)(2,1)S(1)}, u32[]{:S(2)}, u32[]{:S(2)}) collective-permute-start(bf16[512,2048]{1,0:T(8,128)(2,1)S(1)} %branch_2_fun.33.mine), channel_id=1, source_target_pairs={{0,4},{4,0},{8,12},{12,8},{16,20},{20,16},{24,28},{28,24},{1,5},{5... | collective-permute-start | bytes 6291464 | tf_op jit(solution)/shard_map/cond/branch_2_fun/ppermute | solution.py:745
  339.1 14.2 %collective-permute-start.181 = (bf16[320,2048]{1,0:T(8,128)(2,1)S(1)}, bf16[320,2048]{1,0:T(8,128)(2,1)S(1)}, u32[]{:S(2)}, u32[]{:S(2)}) collective-permute-start(bf16[320,2048]{1,0:T(8,128)(2,1)S(1)} %branch_2_fun.34.mine), channel_id=1, source_target_pairs={{0,4},{4,0},{8,12},{12,8},{16,20},{20,16},{24,28},{28,24},{1,5},{5... | collective-permute-start | bytes 3932168 | tf_op jit(solution)/shard_map/cond/branch_2_fun/ppermute | solution.py:745
  (47 other events, 447.7 us)
Sparse Core Ops, SparseCore 0:
  55.5 73.6 all-gather.12
